TPU v7x, 32 devices: a whole 2x2x4 slice. The times are simulated.
32 devices in a mesh: chan: 16 (over z, y, core), freq: 2 (over x).
Axes of the slice: x: 2, y: 2, z: 4, core: 2. Of those that a mesh axis runs over, the one named last changes fastest.
Arguments:
- records: bfloat16 [2048, 64, 512], P('chan', 'freq'), may hold values from -6 to 6
- taper_select: int32 [64], P('freq'), may hold values from 0 to 3
- source_index: int32 [128], replicated, may hold values from 0 to 2047
Outputs:
- correlations: bfloat16 [2048, 128, 256], P('chan', 'freq')
Inputs may be any that keep to these rules, and one draw needn't show every extreme that they name: `source_index`: sources may repeat.
All inputs are finite; a program needn't handle non-finite values.
Results may differ from a plain program's by a relative error of at most 0.0082.
Values may be sent and summed in bfloat16 or wider, within the bound.
A program may use at most 128 MiB of HBM per device.

v0:
```python
import math

import jax
import jax.numpy as jnp
from jax import lax
from jax.sharding import PartitionSpec as P

LAGS = 256


def make_tables(nwin, nfreq, lags):
    n_int = jnp.arange(nwin, dtype=jnp.int32)
    k_int = jnp.arange(nfreq, dtype=jnp.int32)
    phase = (n_int[:, None] * k_int[None, :] % nwin).astype(jnp.float32) * (2.0 * math.pi / nwin)
    dft_table = (
        jnp.concatenate([jnp.cos(phase), -jnp.sin(phase)], axis=1) / math.sqrt(nwin)
    ).astype(jnp.bfloat16)
    sine = jnp.sin(math.pi * (n_int.astype(jnp.float32) + 0.5) / nwin)
    powers = jnp.array([0.5, 1.0, 2.0, 3.0], jnp.float32)
    taper_table = jnp.power(sine[None, :], powers[:, None])
    half = nfreq // 4
    gap = jnp.abs(k_int[:, None] - k_int[None, :])
    band = (gap <= half).astype(jnp.float32)
    lag_int = jnp.arange(lags, dtype=jnp.int32) - lags // 2
    lphase = (k_int[:, None] * lag_int[None, :] % nwin).astype(jnp.float32) * (2.0 * math.pi / nwin)
    weight = jnp.where(k_int == 0, 1.0, 2.0).astype(jnp.float32)[:, None] / math.sqrt(2.0 * nfreq)
    inverse_table = jnp.concatenate(
        [weight * jnp.cos(lphase), -weight * jnp.sin(lphase)], axis=0
    ).astype(jnp.bfloat16)
    return (dft_table, taper_table, band, inverse_table, 2 * half + 1)


def whiten(block, taper, dft_table, band, count):
    chans, segs, nwin = block.shape
    nfreq = nwin // 2
    tapered = (block.astype(jnp.float32) * taper[None, :, :]).astype(jnp.bfloat16)
    spectra = jnp.dot(
        tapered.reshape(chans * segs, nwin), dft_table, preferred_element_type=jnp.float32
    )
    real_part = spectra[:, :nfreq]
    imag_part = spectra[:, nfreq:]
    power = real_part * real_part + imag_part * imag_part
    smooth = jnp.dot(power, band, precision=lax.Precision.HIGHEST) / count
    factor = 1.0 / jnp.sqrt(smooth + 1e-06)
    whitened = jnp.stack([real_part * factor, imag_part * factor], axis=1).astype(jnp.bfloat16)
    return whitened.reshape(chans, segs, 2, nfreq)


def cross_spectra(receivers, sources):
    segs = receivers.shape[1]
    real_r = receivers[:, :, 0, :]
    imag_r = receivers[:, :, 1, :]
    real_s = sources[:, :, 0, :]
    imag_s = sources[:, :, 1, :]
    real_c = jnp.einsum(
        "cgf,sgf->csf", real_r, real_s, preferred_element_type=jnp.float32
    ) + jnp.einsum("cgf,sgf->csf", imag_r, imag_s, preferred_element_type=jnp.float32)
    imag_c = jnp.einsum(
        "cgf,sgf->csf", imag_r, real_s, preferred_element_type=jnp.float32
    ) - jnp.einsum("cgf,sgf->csf", real_r, imag_s, preferred_element_type=jnp.float32)
    return (jnp.stack([real_c, imag_c], axis=2) / math.sqrt(segs)).astype(jnp.bfloat16)


def body(records, taper_select, source_index):
    ch_dev, seg_dev, nwin = records.shape
    nfreq = nwin // 2
    dft_table, taper_table, band, inverse_table, count = make_tables(nwin, nfreq, LAGS)
    chooser = (taper_select[:, None] == jnp.arange(4, dtype=jnp.int32)[None, :]).astype(jnp.float32)
    taper = jnp.dot(chooser, taper_table, precision=lax.Precision.HIGHEST)
    whitened = whiten(records, taper, dft_table, band, count)
    mine = lax.axis_index("chan")
    owner = source_index // ch_dev
    local_row = source_index - owner * ch_dev
    picker = (
        (owner == mine)[:, None]
        & (local_row[:, None] == jnp.arange(ch_dev, dtype=jnp.int32)[None, :])
    ).astype(jnp.bfloat16)
    receivers = lax.all_to_all(whitened, "freq", split_axis=3, concat_axis=1, tiled=True)
    picked = jnp.einsum("sc,cgrf->sgrf", picker, receivers, preferred_element_type=jnp.float32)
    sources = lax.psum(picked.astype(jnp.bfloat16), "chan")
    cross = cross_spectra(receivers, sources)
    regrouped = lax.all_to_all(cross, "freq", split_axis=1, concat_axis=3, tiled=True)
    src_dev = regrouped.shape[1]
    flat = regrouped.reshape(ch_dev * src_dev, 2 * nfreq)
    lagged = jnp.dot(flat, inverse_table, preferred_element_type=jnp.float32)
    return lagged.astype(jnp.bfloat16).reshape(ch_dev, src_dev, LAGS)


def solution(mesh):
    placed = (P("chan", "freq", None), P("freq"), P())
    return jax.shard_map(
        body, mesh=mesh, in_specs=placed, out_specs=P("chan", "freq", None), check_vma=False
    )
```

profile of v0, /device:TPU:0, one launch (start us, length us, event | category | flops | bytes accessed | tf_op | source)
XLA Modules:
  0.0 398.4 jit_solution(15184285262922105914)
XLA Ops:
  6.5 2.1 sine_negate_fusion
  8.7 0.9 fusion.34
  9.6 3.3 multiply_convert_fusion
  12.9 2.4 fusion.12
  15.3 4.5 %multiply_convert_fusion.2 = (bf16[4096,256]{1,0:T(8,128)(2,1)}, bf16[4096,256]{1,0:T(8,128)(2,1)}) fusion(f32[4096,512]{1,0:T(8,128)S(1)} %fusion.12), kind=kOutput, calls=%fused_computation.11 | convolution fusion | flops 3230859264 | bytes 20971520 | tf_op jit(solution)/shard_map/dot_general | solution.py:43
  19.8 4.3 %copy.51 = bf16[128,32,1,256]{0,1,2,3:T(8,128)(2,1)S(1)} copy(bf16[128,32,1,256]{3,1,0,2:T(8,128)(2,1)} %bitcast.47) | data formatting | bytes 4194304 | tf_op jit(solution)/shard_map/stack | solution.py:45
  24.1 5.2 %copy.52 = bf16[128,32,1,256]{0,1,2,3:T(8,128)(2,1)} copy(bf16[128,32,1,256]{3,1,0,2:T(8,128)(2,1)} %bitcast.46) | data formatting | bytes 4194304 | tf_op jit(solution)/shard_map/stack | solution.py:45
  29.2 4.0 pad_maximum_fusion
  33.2 0.0 copy-start.2
  33.2 5.7 %all-to-all-start = ((bf16[128,32,2,256]{0,1,2,3:T(8,128)(2,1)}), bf16[128,32,2,256]{0,1,2,3:T(8,128)(2,1)}, u32[]{:S(2)}, u32[]{:S(2)}) async-start(bf16[128,32,2,256]{0,1,2,3:T(8,128)(2,1)} %pad_maximum_fusion), calls=%async_computation | async-start | bytes 8388608 | tf_op jit(solution)/shard_map/all_to_all | solution.py:78
  38.9 0.2 all-reduce.2.cloned.1.call-start
  39.2 0.0 copy-done.2
  39.2 48.6 %all-to-all-done = bf16[128,32,2,256]{0,1,2,3:T(8,128)(2,1)} async-done(((bf16[128,32,2,256]{0,1,2,3:T(8,128)(2,1)}), bf16[128,32,2,256]{0,1,2,3:T(8,128)(2,1)}, u32[]{:S(2)}, u32[]{:S(2)}) %all-to-all-start) | async-done | bytes 4194336 | tf_op jit(solution)/shard_map/all_to_all | solution.py:78
  87.8 7.9 %copy.53 = bf16[128,32,2,2,128]{4,0,2,1,3:T(8,128)(2,1)} copy(bf16[128,32,2,2,128]{0,1,2,4,3:T(8,128)(2,1)} %bitcast.5) | data formatting | bytes 8388608 | tf_op jit(solution)/shard_map/all_to_all | solution.py:78
  95.6 5.5 %convolution_convert_fusion.1 = bf16[128,64,2,128]{3,0,2,1:T(8,128)(2,1)} fusion(bf16[128,64,2,128]{3,0,2,1:T(8,128)(2,1)} %bitcast.42, s32[128]{0:T(128)S(1)} %multiply_subtract_fusion, pred[128]{0:T(512)(128)(4,1)S(1)} %get-tuple-element.5), kind=kOutput, calls=%fused_computation.17 | convolution fusion | flops 539000832 | bytes 8389248 | tf_op jit(solution)/shard_map/sc,cgrf->sgrf/dot_general | solution.py:79
  101.1 0.0 all-reduce.2.cloned.1.call-update
  101.1 4.0 %slice_bitcast_fusion.2 = (bf16[128,64,128]{2,0,1:T(8,128)(2,1)}, bf16[128,64,128]{2,0,1:T(8,128)(2,1)S(1)}) fusion(bf16[128,64,2,128]{3,0,2,1:T(8,128)(2,1)} %bitcast.43), kind=kLoop, calls=%fused_computation.20 | loop fusion | bytes 8388608 | tf_op jit(solution)/shard_map/squeeze | solution.py:51
  105.1 4.2 %copy.55 = bf16[128,64,128]{0,1,2:T(8,128)(2,1)} copy(bf16[128,64,128]{2,0,1:T(8,128)(2,1)} %get-tuple-element.9) | data formatting | bytes 4194304 | tf_op jit(solution)/shard_map/squeeze | solution.py:51
  109.3 2.8 copy.57
  112.1 101.1 %all-reduce.2.cloned.1.call-done = bf16[128,64,2,128]{3,0,2,1:T(8,128)(2,1)} async-done(((bf16[128,64,2,128]{3,0,2,1:T(8,128)(2,1)}), bf16[128,64,2,128]{3,0,2,1:T(8,128)(2,1)}) %all-reduce.2.cloned.1.call-update) | async-done | bytes 4194320 | tf_op jit(solution)/shard_map/psum | solution.py:80
  213.2 4.0 %slice_bitcast_fusion.1 = (bf16[128,64,128]{2,0,1:T(8,128)(2,1)}, bf16[128,64,128]{2,0,1:T(8,128)(2,1)S(1)}) fusion(bf16[128,64,2,128]{3,0,2,1:T(8,128)(2,1)} %all-reduce.2.cloned.1.call-done), kind=kLoop, calls=%fused_computation.19 | loop fusion | bytes 8388608 | tf_op jit(solution)/shard_map/squeeze | solution.py:54
  217.2 2.9 copy.54
  220.1 3.3 copy.56
  223.4 0.0 copy-start
  223.4 0.0 copy-start.1
  223.4 3.7 fusion.45
  227.1 0.0 copy-done
  227.1 0.0 copy-done.1
  227.1 1.3 fusion.46
  228.5 3.0 add_bitcast_fusion
  231.5 3.0 subtract_bitcast_fusion
  234.5 4.4 %fusion = bf16[128,128,2,128]{0,1,3,2:T(8,128)(2,1)} fusion(f32[128,128,1,128]{0,1,3,2:T(8,128)S(1)} %subtract_bitcast_fusion, f32[128,128,1,128]{0,1,3,2:T(8,128)S(1)} %add_bitcast_fusion), kind=kLoop, calls=%fused_computation.1 | loop fusion | flops 12582912 | bytes 25165824 | tf_op jit(solution)/shard_map/convert_element_type | solution.py:61
  238.9 12.0 %copy.62 = bf16[128,128,2,128]{0,3,2,1:T(8,128)(2,1)} copy(bf16[128,128,2,128]{0,1,3,2:T(8,128)(2,1)} %fusion) | data formatting | bytes 16777216 | tf_op jit(solution)/shard_map/convert_element_type | solution.py:61
  250.9 6.9 %all-to-all-start.1 = ((bf16[128,128,2,128]{0,3,2,1:T(8,128)(2,1)}), bf16[128,128,2,128]{0,3,2,1:T(8,128)(2,1)}, u32[]{:S(2)}, u32[]{:S(2)}) async-start(bf16[128,128,2,128]{0,3,2,1:T(8,128)(2,1)} %copy.62), calls=%async_computation.1 | async-start | bytes 16777216 | tf_op jit(solution)/shard_map/all_to_all | solution.py:82
  257.9 1.2 multiply_convert_fusion.4
  259.1 90.3 %all-to-all-done.1 = bf16[128,128,2,128]{0,3,2,1:T(8,128)(2,1)} async-done(((bf16[128,128,2,128]{0,3,2,1:T(8,128)(2,1)}), bf16[128,128,2,128]{0,3,2,1:T(8,128)(2,1)}, u32[]{:S(2)}, u32[]{:S(2)}) %all-to-all-start.1) | async-done | bytes 8388640 | tf_op jit(solution)/shard_map/all_to_all | solution.py:82
  349.3 21.3 %copy.63 = bf16[128,2,64,2,128]{4,1,3,2,0:T(2,128)(2,1)} copy(bf16[128,2,64,2,128]{0,4,3,2,1:T(8,128)(2,1)} %bitcast.17) | data formatting | bytes 16777216 | tf_op jit(solution)/shard_map/all_to_all | solution.py:82
  370.7 13.1 %reshape.45 = bf16[8192,512]{1,0:T(8,128)(2,1)} reshape(bf16[128,64,2,2,128]{4,3,2,1,0:T(2,128)(2,1)} %bitcast.44) | data formatting | bytes 16777216 | tf_op jit(solution)/shard_map/reshape | solution.py:84
  383.8 7.7 %convolution_convert_fusion = bf16[8192,256]{1,0:T(8,128)(2,1)} fusion(bf16[8192,512]{1,0:T(8,128)(2,1)} %reshape.45, bf16[256,256]{1,0:T(8,128)(2,1)S(1)} %get-tuple-element.14, bf16[256,256]{1,0:T(8,128)(2,1)S(1)} %get-tuple-element.13), kind=kOutput, calls=%fused_computation.2 | convolution fusion | flops 2150105088 | bytes 12845056 | tf_op jit(solution)/shard_map/dot_general | solution.py:85
  (5 shorter events, 0.1 us)
Async XLA Ops:
  33.2 6.0 %copy-start.2 = (s32[128]{0:T(128)S(1)}, s32[128]{0:T(128)}, u32[]{:S(2)}) copy-start(s32[128]{0:T(128)} %param.6) | copy-start | bytes 1540
  33.2 54.6 %all-to-all-start = ((bf16[128,32,2,256]{0,1,2,3:T(8,128)(2,1)}), bf16[128,32,2,256]{0,1,2,3:T(8,128)(2,1)}, u32[]{:S(2)}, u32[]{:S(2)}) async-start(bf16[128,32,2,256]{0,1,2,3:T(8,128)(2,1)} %pad_maximum_fusion), calls=%async_computation | async-start | bytes 8388608 | tf_op jit(solution)/shard_map/all_to_all | solution.py:78
  38.9 174.3 %all-reduce.2.cloned.1.call-start = ((), (), s32[]{:S(2)}) async-start(), calls=%async_computation.2 | async-start | bytes 8388608 | tf_op jit(solution)/shard_map/psum | solution.py:80
  223.4 3.7 copy-start
  223.4 3.7 copy-start.1
  250.9 98.4 %all-to-all-start.1 = ((bf16[128,128,2,128]{0,3,2,1:T(8,128)(2,1)}), bf16[128,128,2,128]{0,3,2,1:T(8,128)(2,1)}, u32[]{:S(2)}, u32[]{:S(2)}) async-start(bf16[128,128,2,128]{0,3,2,1:T(8,128)(2,1)} %copy.62), calls=%async_computation.1 | async-start | bytes 16777216 | tf_op jit(solution)/shard_map/all_to_all | solution.py:82
Sparse Core Ops, SparseCore 0:
  101.2 111.9 all-reduce.1
where the time goes:
time: 400 us; the launch traced here: 398 us
  waiting for transfers between devices  240 us (60%)
  local copies, waits for them, and re-layouts  85 us (21%)
  matrix products  32 us (8%)
  other arithmetic  15 us (4%)
  between operations  13.6 us (3%)
  starting transfers between devices  12.9 us (3%)
    psum x1, waiting for transfers between devices, body(): sources = lax.psum(picked.astype(jnp.bfloat16), 'chan')  101 us
    all_to_all x1, waiting for transfers between devices, body(): lax.all_to_all(cross, 'freq', split_axis=1, concat_axis=3, tiled=True)  90.3 us
    all_to_all x1, waiting for transfers between devices, body(): lax.all_to_all(whitened, 'freq', split_axis=3, concat_axis=1, tiled=True)  48.6 us
    all_to_all x1, local copies, waits for them, and re-layouts, body(): lax.all_to_all(cross, 'freq', split_axis=1, concat_axis=3, tiled=True)  21.3 us
    reshape x1, local copies, waits for them, and re-layouts, body(): flat = regrouped.reshape(ch_dev * src_dev, 2 * nfreq)  13.1 us
    convert_element_type x1, local copies, waits for them, and re-layouts, cross_spectra(): (jnp.stack([real_c, imag_c], axis=2) / math.sqrt(segs)).astype(jnp.bfloat16)  12 us
    another operation x2, local copies, waits for them, and re-layouts, whiten(): jnp.stack([real_part * factor, imag_part * factor], axis=1)  9.46 us
    squeeze x2, local copies, waits for them, and re-layouts, cross_spectra(): real_r = receivers[:, :, 0, :]  8.23 us
  transfers between devices with their start and end apart: 3, of which 3 were waited for; matrix products, arithmetic and copies ran while one was open for 3% of the time, Pallas kernels for 0%

commit v1 on v0

v1 whole, which is shorter than its diff:
```python
import functools
import math

import jax
import jax.numpy as jnp
import ml_dtypes
import numpy as np
from jax import lax
from jax.experimental import pallas as pl
from jax.experimental.pallas import tpu as pltpu
from jax.sharding import PartitionSpec as P

LAGS = 256
STEP = 16
F32 = jnp.float32
BF16 = jnp.bfloat16


def make_tables(nwin, nfreq, lags):
    n_int = np.arange(nwin)
    k_int = np.arange(nfreq)
    phase = (n_int[:, None] * k_int[None, :] % nwin) * (2.0 * math.pi / nwin)
    dft = np.concatenate([np.cos(phase), -np.sin(phase)], axis=1) / math.sqrt(nwin)
    sine = np.sin(math.pi * (n_int + 0.5) / nwin)
    taper = np.power(sine[None, :], np.array([0.5, 1.0, 2.0, 3.0])[:, None])
    half = nfreq // 4
    band = np.abs(k_int[:, None] - k_int[None, :]) <= half
    lag_int = np.arange(lags) - lags // 2
    lphase = (k_int[:, None] * lag_int[None, :] % nwin) * (2.0 * math.pi / nwin)
    weight = np.where(k_int == 0, 1.0, 2.0)[:, None] / math.sqrt(2.0 * nfreq)
    inverse = np.concatenate([weight * np.cos(lphase), -weight * np.sin(lphase)], axis=0)
    low = ml_dtypes.bfloat16
    return (
        dft.T.astype(np.float32).astype(low),
        taper.astype(np.float32),
        band.astype(low),
        inverse.T.astype(np.float32).astype(low),
        2 * half + 1,
    )


def pick_kernel(owned_ref, row_ref, x_ref, o_ref):
    def one(s, carry):
        keep = jnp.where(owned_ref[s] == 1, 1.0, 0.0).astype(BF16)
        o_ref[s] = x_ref[row_ref[s]] * keep
        return carry

    lax.fori_loop(0, o_ref.shape[0], one, 0)


def pick(records, owned, rows):
    count = rows.shape[0]
    smem = pl.BlockSpec(memory_space=pltpu.SMEM)
    vmem = pl.BlockSpec(memory_space=pltpu.VMEM)
    return pl.pallas_call(
        pick_kernel,
        out_shape=jax.ShapeDtypeStruct((count,) + records.shape[1:], BF16),
        in_specs=[smem, smem, vmem],
        out_specs=vmem,
        compiler_params=pltpu.CompilerParams(vmem_limit_bytes=40 << 20),
        name="pick",
    )(owned, rows, records)


def whiten_kernel(count, x_ref, t_ref, dft_ref, band_ref, o_ref, xf, of):
    chans, segs, nwin = x_ref.shape
    nfreq = nwin // 2
    lane = 128
    for q in range(nwin // lane):
        cols = slice(q * lane, (q + 1) * lane)
        x = x_ref[:, :, cols].astype(F32) * t_ref[:, cols][None]
        xf[q] = x.reshape(chans * segs, lane)
    for p in range(segs // 2):
        pair = []
        for g in (2 * p, 2 * p + 1):
            parts = [xf[q, pl.ds(g, chans, stride=segs), :] for q in range(nwin // lane)]
            pair.append(jnp.concatenate(parts, axis=1).astype(BF16))
        both = jnp.concatenate(pair, axis=0)
        spectra = lax.dot_general(
            dft_ref[...], both, (((1,), (1,)), ((), ())), preferred_element_type=F32
        )
        real, imag = spectra[:nfreq], spectra[nfreq:]
        power = real * real + imag * imag
        high = power.astype(BF16)
        low = (power - high.astype(F32)).astype(BF16)
        smooth = jnp.dot(band_ref[...], high, preferred_element_type=F32)
        smooth += jnp.dot(band_ref[...], low, preferred_element_type=F32)
        factor = lax.rsqrt(smooth * (1.0 / count) + 1e-06)
        real, imag = real * factor, imag * factor
        for j in range(2):
            cols = slice(j * chans, (j + 1) * chans)
            of[pl.ds(2 * p + j, nfreq, stride=2 * segs), :] = real[:, cols]
            of[pl.ds(segs + 2 * p + j, nfreq, stride=2 * segs), :] = imag[:, cols]
    o_ref[...] = of[...].reshape(nfreq, 2, segs, chans).astype(BF16)


def whiten_across(records, taper, dft, band, count):
    chans, segs, nwin = records.shape
    nfreq = nwin // 2
    return pl.pallas_call(
        functools.partial(whiten_kernel, count),
        out_shape=jax.ShapeDtypeStruct((nfreq, 2, segs, chans), BF16),
        grid=(segs // STEP,),
        in_specs=[
            pl.BlockSpec((chans, STEP, nwin), lambda i: (0, i, 0)),
            pl.BlockSpec((STEP, nwin), lambda i: (i, 0)),
            pl.BlockSpec((nwin, nwin), lambda i: (0, 0)),
            pl.BlockSpec((nfreq, nfreq), lambda i: (0, 0)),
        ],
        out_specs=pl.BlockSpec((nfreq, 2, STEP, chans), lambda i: (0, 0, i, 0)),
        scratch_shapes=[
            pltpu.VMEM((nwin // 128, chans * STEP, 128), F32),
            pltpu.VMEM((nfreq * 2 * STEP, chans), F32),
        ],
        compiler_params=pltpu.CompilerParams(vmem_limit_bytes=48 << 20),
        cost_estimate=pl.CostEstimate(
            flops=4 * chans * segs * nwin * nwin,
            bytes_accessed=4 * chans * segs * nwin,
            transcendentals=0,
        ),
        name="whiten_across",
    )(records, taper, dft, band)


def whiten_rows(block, taper, dft, band, count):
    nfreq = block.shape[-1] // 2
    tapered = (block.astype(F32) * taper).astype(BF16)
    spectra = lax.dot_general(
        tapered, dft, (((tapered.ndim - 1,), (1,)), ((), ())), preferred_element_type=F32
    )
    real, imag = spectra[..., :nfreq], spectra[..., nfreq:]
    power = real * real + imag * imag
    high = power.astype(BF16)
    low = (power - high.astype(F32)).astype(BF16)
    smooth = jnp.dot(high, band, preferred_element_type=F32)
    smooth += jnp.dot(low, band, preferred_element_type=F32)
    factor = lax.rsqrt(smooth / count + 1e-06)
    return jnp.stack([real * factor, imag * factor], axis=-2).astype(BF16)


def cross_kernel(nf, scale, *refs):
    *r_refs, s_ref, inv_ref, o_ref, zs, os = refs
    fb, srcs, depth = s_ref.shape
    nfreq2 = inv_ref.shape[1]
    nfreq = nfreq2 // 2
    chans, group, lags = o_ref.shape
    half = depth // 2
    step = pl.program_id(0)

    @pl.when(step < nf)
    def _():
        for j in range(fb):
            parts = []
            for part in range(2):
                for r in r_refs:
                    parts.append(r[j, part])
            receivers = jnp.concatenate(parts, axis=0)
            s = s_ref[j]
            turned = jnp.concatenate([-s[:, half:], s[:, :half]], axis=1)
            both = jnp.concatenate([s, turned], axis=0)
            cross = jnp.dot(both, receivers, preferred_element_type=F32) * scale
            f = step * fb + j
            zs[pl.ds(f, srcs, stride=nfreq2), :] = cross[:srcs]
            zs[pl.ds(nfreq + f, srcs, stride=nfreq2), :] = cross[srcs:]

    @pl.when(step >= nf)
    def _():
        first = (step - nf) * group
        for p in range(group // 2):
            pair = []
            for t in (2 * p, 2 * p + 1):
                row = pl.multiple_of((first + t) * nfreq2, nfreq2)
                pair.append(zs[pl.ds(row, nfreq2), :].astype(BF16))
            lagged = jnp.dot(
                inv_ref[...], jnp.concatenate(pair, axis=1), preferred_element_type=F32
            )
            turned = lagged.T
            for t in range(2):
                for q in range(lags // 128):
                    os[q, pl.ds(2 * p + t, chans, stride=group), :] = turned[
                        t * chans : (t + 1) * chans, q * 128 : (q + 1) * 128
                    ]
        for q in range(lags // 128):
            o_ref[:, :, q * 128 : (q + 1) * 128] = (
                os[q].reshape(chans, group, 128).astype(BF16)
            )


def cross_lags(receivers, sources, inverse, scale):
    nfreq, srcs, depth = sources.shape
    chans = receivers[0].shape[-1]
    lags = inverse.shape[0]
    fb = 16
    nf = nfreq // fb
    group = min(16, srcs)
    ns = srcs // group
    r_specs = [
        pl.BlockSpec((fb,) + r.shape[1:], lambda i: (jnp.minimum(i, nf - 1), 0, 0, 0))
        for r in receivers
    ]
    return pl.pallas_call(
        functools.partial(cross_kernel, nf, scale),
        out_shape=jax.ShapeDtypeStruct((chans, srcs, lags), BF16),
        grid=(nf + ns,),
        in_specs=r_specs
        + [
            pl.BlockSpec((fb, srcs, depth), lambda i: (jnp.minimum(i, nf - 1), 0, 0)),
            pl.BlockSpec(inverse.shape, lambda i: (0, 0)),
        ],
        out_specs=pl.BlockSpec((chans, group, lags), lambda i: (0, jnp.maximum(i - nf, 0), 0)),
        scratch_shapes=[
            pltpu.VMEM((srcs * 2 * nfreq, chans), F32),
            pltpu.VMEM((lags // 128, chans * group, 128), F32),
        ],
        compiler_params=pltpu.CompilerParams(vmem_limit_bytes=56 << 20),
        name="cross_lags",
    )(*receivers, sources, inverse)


def body(n, m, records, taper_select, source_index):
    chans, segs, nwin = records.shape
    nfreq = nwin // 2
    nsrc = source_index.shape[0]
    per = nsrc // n
    share = -(-per // m)
    dft, taper_table, band, inverse, count = make_tables(nwin, nfreq, LAGS)
    me = lax.axis_index("freq")
    mine = lax.axis_index("chan")

    def from_ahead(value, d):
        return lax.ppermute(value, "freq", [(q, (q - d) % n) for q in range(n)])

    def taper_of(select):
        out = jnp.where((select == 0)[:, None], taper_table[0], taper_table[1])
        out = jnp.where((select == 2)[:, None], taper_table[2], out)
        return jnp.where((select == 3)[:, None], taper_table[3], out)

    arrived = []
    for d in range(1, n):
        select = from_ahead(taper_select, d)
        for at in range(0, segs, STEP):
            block = from_ahead(lax.slice_in_dim(records, at, at + STEP, axis=1), d)
            arrived.append((block, select[at : at + STEP]))

    index = jnp.pad(source_index.reshape(n, per), ((0, 0), (0, share * m - per)), constant_values=-1)
    index = index.reshape(n, m, share).transpose(1, 0, 2).reshape(-1)
    rows = index - mine * chans
    owned = (rows >= 0) & (rows < chans) & (index >= 0)
    rows = jnp.clip(rows, 0, chans - 1)
    picked = pick(records, owned.astype(jnp.int32), rows.astype(jnp.int32))
    own_sources = lax.psum_scatter(picked, "chan", scatter_dimension=0, tiled=True)
    own_taper = taper_of(taper_select)
    spectra = whiten_rows(own_sources, own_taper[None], dft, band, count)
    spectra = spectra.reshape(n, share, segs, 2, nfreq).transpose(0, 4, 1, 3, 2)
    pieces = []
    for d in range(n):
        give = lax.dynamic_index_in_dim(spectra, (me - d) % n, 0, keepdims=False)
        pieces.append(from_ahead(give, d) if d else give)
    small = jnp.stack(pieces, axis=3).reshape(nfreq, share, 2 * n * segs)
    gathered = lax.all_gather(small, "chan", axis=1, tiled=True)
    sources = gathered[:, :per]

    receivers = [whiten_across(records, own_taper, dft, band, count)]
    for block, select in arrived:
        receivers.append(whiten_across(block, taper_of(select), dft, band, count))
    return cross_lags(receivers, sources, inverse, 1.0 / math.sqrt(n * segs))


def solution(mesh):
    placed = (P("chan", "freq", None), P("freq"), P())
    return jax.shard_map(
        functools.partial(body, mesh.shape["freq"], mesh.shape["chan"]),
        mesh=mesh,
        in_specs=placed,
        out_specs=P("chan", "freq", None),
        check_vma=False,
    )
```

time: 400 us -> 249 us (0.62)
  waiting for transfers between devices: 240 us -> 145 us
  local copies, waits for them, and re-layouts: 85 us -> 20.3 us
  Pallas kernels: 0 us -> 61 us
  matrix products: 32 us -> 1.69 us
  other arithmetic: 15 us -> 1.62 us
  starting transfers between devices: 12.9 us -> 5.11 us
    all_to_all x2 -> x0, waiting for transfers between devices: 139 us -> none  [the longest x1 90.3 us: body(): lax.all_to_all(cross, 'freq', split_axis=1, concat_axis=3, tiled=True)]
    psum x1 -> x0, waiting for transfers between devices: 101 us -> none  [body(): sources = lax.psum(picked.astype(jnp.bfloat16), 'chan')]
    reduce_scatter x0 -> x1, waiting for transfers between devices: none -> 74.8 us  [body(): lax.psum_scatter(picked, 'chan', scatter_dimension=0, tiled=True)]
    ppermute x0 -> x4, waiting for transfers between devices: none -> 70.3 us  [from_ahead(): return lax.ppermute(value, 'freq', [(q, (q - d) % n) for q in range(n)])]
    pallas_call x0 -> x5, Pallas kernels: none -> 61 us  [the longest x3 32 us: whiten_across(): pl.pallas_call(functools.partial(whiten_kernel, count), out_shape=jax.Sha...]
    dot_general x9 -> x3, matrix products: 32 us -> 1.69 us  [the longest x1 1.28 us: whiten_rows(): lax.dot_general(tapered, dft, (((tapered.ndim - 1,), (1,)), ((), ())), pr...]
    all_to_all x2 -> x0, local copies, waits for them, and re-layouts: 29.2 us -> none  [the longest x1 21.3 us: body(): lax.all_to_all(cross, 'freq', split_axis=1, concat_axis=3, tiled=True)]
    squeeze x6 -> x0, local copies, waits for them, and re-layouts: 21.2 us -> none  [the longest x2 8.23 us: cross_spectra(): real_r = receivers[:, :, 0, :]]
  transfers between devices with their start and end apart: 3 -> 6, of which waited for: 3 -> 3; matrix products, arithmetic and copies ran while one was open for 3% -> 1% of each run, Pallas kernels for 0% -> 13%
where the time goes in v1:
time: 249 us; the launch traced here: 248 us
  waiting for transfers between devices  145 us (58%)
  Pallas kernels  61 us (24%)
  local copies, waits for them, and re-layouts  20.3 us (8%)
  between operations  13.7 us (6%)
  starting transfers between devices  5.11 us (2%)
    reduce_scatter x1, waiting for transfers between devices, body(): lax.psum_scatter(picked, 'chan', scatter_dimension=0, tiled=True)  74.8 us
    ppermute x4, waiting for transfers between devices, from_ahead(): return lax.ppermute(value, 'freq', [(q, (q - d) % n) for q in range(n)])  70.3 us
    pallas_call x3, Pallas kernels, whiten_across(): pl.pallas_call(functools.partial(whiten_kernel, count), out_shape=jax.Sha...  32 us
    pallas_call x1, Pallas kernels, cross_lags(): pl.pallas_call(functools.partial(cross_kernel, nf, scale), out_shape=jax....  26.8 us
    unnamed x28, local copies, waits for them, and re-layouts  9.43 us
    all_gather x1, local copies, waits for them, and re-layouts, body(): gathered = lax.all_gather(small, 'chan', axis=1, tiled=True)  6.86 us
    ppermute x4, starting transfers between devices, from_ahead(): return lax.ppermute(value, 'freq', [(q, (q - d) % n) for q in range(n)])  5.06 us
  transfers between devices with their start and end apart: 6, of which 3 were waited for; matrix products, arithmetic and copies ran while one was open for 1% of the time, Pallas kernels for 13%

profile of v1, /device:TPU:0, one launch (start us, length us, event | category | flops | bytes accessed | tf_op | source)
XLA Modules:
  0.0 248.5 jit_solution(6773774293604188705)
XLA Ops:
  6.5 0.0 reduce-scatter.2.cloned.1.call-start
  6.5 0.7 and_convert_fusion
  7.2 0.7 subtract_clamp_fusion
  7.9 0.1 min.16
  8.0 0.1 min.18.row_ref
  8.1 0.1 reshape.134
  8.2 0.1 reshape.132.owned_ref
  8.3 0.0 copy-start
  8.3 2.2 copy-done
  10.5 2.3 pick.1
  12.8 0.0 copy-start.1
  12.8 2.0 copy-done.1
  14.8 0.0 copy-start.13
  14.8 0.0 copy-start.9
  14.8 0.0 copy-start.10
  14.8 0.0 copy-start.11
  14.8 0.0 copy-start.12
  14.9 0.0 copy-start.7
  14.9 0.0 copy-start.8
  14.9 0.0 reduce-scatter.2.cloned.1.call-update
  14.9 0.0 all-gather.2.cloned.1.call-start
  15.0 0.5 copy-done.13
  15.5 0.0 copy-done.9
  15.5 0.0 copy-done.10
  15.6 0.0 copy-done.11
  15.6 0.0 copy-done.12
  15.6 0.1 select_select_fusion.t_ref
  15.7 74.8 %reduce-scatter.2.cloned.1.call-done = bf16[8,32,512]{2,1,0:T(8,128)(2,1)} async-done(((bf16[128,32,512]{2,1,0:T(8,128)(2,1)}), bf16[8,32,512]{2,1,0:T(8,128)(2,1)}) %reduce-scatter.2.cloned.1.call-update) | async-done | bytes 262160 | tf_op jit(solution)/shard_map/reduce_scatter | solution.py:251
  90.4 0.0 copy-done.7
  90.4 1.3 fusion.3
  91.7 0.0 copy-done.8
  91.7 0.2 fusion.10
  91.9 0.2 multiply_convert_fusion.2
  92.2 1.5 collective-permute-start.3
  93.7 3.5 %collective-permute-done.3 = bf16[256,4,2,32]{0,3,2,1:T(8,128)(2,1)S(1)} collective-permute-done((bf16[256,4,2,32]{0,3,2,1:T(8,128)(2,1)S(1)}, bf16[256,4,2,32]{0,3,2,1:T(8,128)(2,1)S(1)}, u32[]{:S(2)}, u32[]{:S(2)}) %collective-permute-start.3) | collective-permute-done | bytes 131104 | tf_op jit(solution)/shard_map/ppermute | solution.py:231
  97.3 0.8 copy.33
  98.1 0.0 all-gather.2.cloned.1.call-update
  98.1 0.0 copy-start.5
  98.1 0.0 copy-start.6
  98.2 2.8 %fusion.12 = (bf16[128,16,512]{2,1,0:T(8,128)(2,1)S(1)}, bf16[128,16,512]{2,1,0:T(8,128)(2,1)S(1)}) fusion(bf16[128,32,512]{2,1,0:T(8,128)(2,1)} %x_ref.3), kind=kLoop, calls=%fused_computation.37 | loop fusion | bytes 8388608 | tf_op jit(solution)/shard_map/slice | solution.py:242
  100.9 1.5 collective-permute-start.2
  102.4 0.6 collective-permute-start
  103.0 1.5 collective-permute-start.1
  104.5 0.0 copy-done.5
  104.5 0.0 copy-done.6
  104.5 17.2 %whiten_across.3.refs_0_ = bf16[256,2,32,128]{3,2,1,0:T(8,128)(2,1)S(1)} custom-call(bf16[128,32,512]{2,1,0:T(8,128)(2,1)} %x_ref.3, f32[32,512]{1,0:T(8,128)S(1)} %select_select_fusion.t_ref, bf16[512,512]{1,0:T(8,128)(2,1)S(1)} %copy-done.5, bf16[256,256]{1,0:T(8,128)(2,1)S(1)} %copy-done.6), custom_call_target="tpu_custom_call" | custom-call | flops 4294967296 | bytes 8388608 | tf_op jit(solution)/shard_map/whiten_across/pallas_call | solution.py:100
  121.7 0.0 copy-start.2
  121.7 2.0 copy-done.2
  123.7 66.8 %collective-permute-done.1 = s32[32]{0:T(128)S(1)} collective-permute-done((s32[32]{0:T(128)S(1)}, s32[32]{0:T(128)S(1)}, u32[]{:S(2)}, u32[]{:S(2)}) %collective-permute-start.1) | collective-permute-done | bytes 160 | tf_op jit(solution)/shard_map/ppermute | solution.py:231
  190.4 0.1 broadcast_compare_fusion.4
  190.5 0.1 select_select_fusion.1
  190.6 0.0 collective-permute-done.2.x_ref
  190.6 7.3 %whiten_across.5.refs_2_ = bf16[256,2,16,128]{3,2,1,0:T(8,128)(2,1)S(1)} custom-call(bf16[128,16,512]{2,1,0:T(8,128)(2,1)S(1)} %collective-permute-done.2.x_ref, f32[16,512]{1,0:T(8,128)S(1)} %get-tuple-element.11.t_ref, bf16[512,512]{1,0:T(8,128)(2,1)S(1)} %copy-done.5, bf16[256,256]{1,0:T(8,128)(2,1)S(1)} %copy-done.6), custom_call_target="tpu_custom_call" | custom-call | flops 2147483648 | bytes 4194304 | tf_op jit(solution)/shard_map/whiten_across/pallas_call | solution.py:100
  197.9 0.0 copy-start.3
  197.9 1.3 copy-done.3
  199.2 0.0 collective-permute-done.x_ref
  199.2 7.5 %whiten_across.4.refs_1_ = bf16[256,2,16,128]{3,2,1,0:T(8,128)(2,1)S(1)} custom-call(bf16[128,16,512]{2,1,0:T(8,128)(2,1)S(1)} %collective-permute-done.x_ref, f32[16,512]{1,0:T(8,128)S(1)} %get-tuple-element.12.t_ref, bf16[512,512]{1,0:T(8,128)(2,1)S(1)} %copy-done.5, bf16[256,256]{1,0:T(8,128)(2,1)S(1)} %copy-done.6), custom_call_target="tpu_custom_call" | custom-call | flops 2147483648 | bytes 4194304 | tf_op jit(solution)/shard_map/whiten_across/pallas_call | solution.py:100
  206.7 0.0 copy-start.4
  206.7 1.3 copy-done.4
  208.0 0.0 all-gather.2.cloned.1.call-done
  208.0 6.9 %copy.34.refs_3_ = bf16[256,64,128]{2,1,0:T(8,128)(2,1)} copy(bf16[256,64,128]{2,0,1:T(8,128)(2,1)} %all-gather.2.cloned.1.call-done) | data formatting | bytes 8388608 | tf_op jit(solution)/shard_map/all_gather | solution.py:260
  214.9 26.8 %cross_lags.1 = bf16[128,64,256]{2,1,0:T(8,128)(2,1)} custom-call(bf16[256,2,32,128]{3,2,1,0:T(8,128)(2,1)} %copy-done.2, bf16[256,2,16,128]{3,2,1,0:T(8,128)(2,1)} %copy-done.4, bf16[256,2,16,128]{3,2,1,0:T(8,128)(2,1)} %copy-done.3, bf16[256,64,128]{2,1,0:T(8,128)(2,1)} %copy.34.refs_3_, bf16[256,512]{1,0:T(8,128)(2,1)} %constant.74.clone.refs_4_), custom_call_target="tpu_custom_call" | custom-call | tf_op jit(solution)/shard_map/cross_lags/pallas_call | solution.py:201
  (5 shorter events, 0.1 us)
Async XLA Ops:
  6.5 83.9 %reduce-scatter.2.cloned.1.call-start = ((), (), s32[]{:S(2)}) async-start(), calls=%async_computation.1 | async-start | bytes 4456448 | tf_op jit(solution)/shard_map/reduce_scatter | solution.py:251
  8.3 2.2 copy-start
  12.8 2.0 copy-start.1
  14.8 0.7 copy-start.13
  14.8 0.7 copy-start.9
  14.8 0.7 copy-start.10
  14.8 0.7 copy-start.11
  14.8 0.7 copy-start.12
  14.9 75.6 %copy-start.7 = (bf16[512,512,1]{1,0,2:T(8,128)(2,1)S(1)}, bf16[512,512,1]{1,0,2:T(8,128)(2,1)}, u32[]{:S(2)}) copy-start(bf16[512,512,1]{1,0,2:T(8,128)(2,1)} %constant.75) | copy-start | bytes 1572868
  14.9 76.8 %copy-start.8 = (bf16[256,256,1]{1,0,2:T(8,128)(2,1)S(1)}, bf16[256,256,1]{1,0,2:T(8,128)(2,1)}, u32[]{:S(2)}) copy-start(bf16[256,256,1]{1,0,2:T(8,128)(2,1)} %constant.76) | copy-start | bytes 393220
  14.9 193.1 %all-gather.2.cloned.1.call-start = ((), (), s32[]{:S(2)}) async-start(), calls=%async_computation.2 | async-start | bytes 4456448 | tf_op jit(solution)/shard_map/all_gather | solution.py:260
  92.2 5.0 %collective-permute-start.3 = (bf16[256,4,2,32]{0,3,2,1:T(8,128)(2,1)S(1)}, bf16[256,4,2,32]{0,3,2,1:T(8,128)(2,1)S(1)}, u32[]{:S(2)}, u32[]{:S(2)}) collective-permute-start(bf16[256,4,2,32]{0,3,2,1:T(8,128)(2,1)S(1)} %get-tuple-element.10), channel_id=1, source_target_pairs={{0,1},{1,0},{2,3},{3,2},{4,5},{5,4},{6,7},{7,6},{8,9},{9,8},{10,11... | collective-permute-start | bytes 393224 | tf_op jit(solution)/shard_map/ppermute | solution.py:231
  98.1 6.3 %copy-start.5 = (bf16[512,512]{1,0:T(8,128)(2,1)S(1)}, bf16[512,512]{1,0:T(8,128)(2,1)}, u32[]{:S(2)}) copy-start(bf16[512,512]{1,0:T(8,128)(2,1)} %constant.72.clone.dft_ref) | copy-start | bytes 1572868
  98.1 6.3 %copy-start.6 = (bf16[256,256]{1,0:T(8,128)(2,1)S(1)}, bf16[256,256]{1,0:T(8,128)(2,1)}, u32[]{:S(2)}) copy-start(bf16[256,256]{1,0:T(8,128)(2,1)} %constant.73.clone.band_ref) | copy-start | bytes 393220
  100.9 89.7 %collective-permute-start.2 = (bf16[128,16,512]{2,1,0:T(8,128)(2,1)S(1)}, bf16[128,16,512]{2,1,0:T(8,128)(2,1)S(1)}, u32[]{:S(2)}, u32[]{:S(2)}) collective-permute-start(bf16[128,16,512]{2,1,0:T(8,128)(2,1)S(1)} %get-tuple-element.5), channel_id=1, source_target_pairs={{0,1},{1,0},{2,3},{3,2},{4,5},{5,4},{6,7},{7,6},{8,9},{9,8},{10,11... | collective-permute-start | bytes 6291464 | tf_op jit(solution)/shard_map/ppermute | solution.py:231
  102.4 96.8 %collective-permute-start = (bf16[128,16,512]{2,1,0:T(8,128)(2,1)S(1)}, bf16[128,16,512]{2,1,0:T(8,128)(2,1)S(1)}, u32[]{:S(2)}, u32[]{:S(2)}) collective-permute-start(bf16[128,16,512]{2,1,0:T(8,128)(2,1)S(1)} %get-tuple-element.6), channel_id=1, source_target_pairs={{0,1},{1,0},{2,3},{3,2},{4,5},{5,4},{6,7},{7,6},{8,9},{9,8},{10,11... | collective-permute-start | bytes 6291464 | tf_op jit(solution)/shard_map/ppermute | solution.py:231
  103.0 87.4 %collective-permute-start.1 = (s32[32]{0:T(128)S(1)}, s32[32]{0:T(128)S(1)}, u32[]{:S(2)}, u32[]{:S(2)}) collective-permute-start(s32[32]{0:T(128)S(1)} %copy-done.13), channel_id=1, source_target_pairs={{0,1},{1,0},{2,3},{3,2},{4,5},{5,4},{6,7},{7,6},{8,9},{9,8},{10,11... | collective-permute-start | bytes 392 | tf_op jit(solution)/shard_map/ppermute | solution.py:231
  121.7 2.0 copy-start.2
  197.9 1.3 copy-start.3
  206.7 1.3 copy-start.4
Sparse Core Ops, SparseCore 0:
  15.0 75.3 reduce-scatter.1
  98.2 49.8 all-gather.1

commit v2 on v1

--- a/solution.py
+++ b/solution.py
@@ -250,6 +250,9 @@
     picked = pick(records, owned.astype(jnp.int32), rows.astype(jnp.int32))
     own_sources = lax.psum_scatter(picked, "chan", scatter_dimension=0, tiled=True)
     own_taper = taper_of(taper_select)
+    receivers = [whiten_across(records, own_taper, dft, band, count)]
+    blocks = [block for block, _ in arrived]
+    own_sources, receivers, blocks = lax.optimization_barrier((own_sources, receivers, blocks))
     spectra = whiten_rows(own_sources, own_taper[None], dft, band, count)
     spectra = spectra.reshape(n, share, segs, 2, nfreq).transpose(0, 4, 1, 3, 2)
     pieces = []
@@ -260,8 +263,7 @@
     gathered = lax.all_gather(small, "chan", axis=1, tiled=True)
     sources = gathered[:, :per]
 
-    receivers = [whiten_across(records, own_taper, dft, band, count)]
-    for block, select in arrived:
+    for block, (_, select) in zip(blocks, arrived):
         receivers.append(whiten_across(block, taper_of(select), dft, band, count))
     return cross_lags(receivers, sources, inverse, 1.0 / math.sqrt(n * segs))
 

time: 249 us -> 214 us (0.86)
  waiting for transfers between devices: 145 us -> 106 us
    reduce_scatter x1, waiting for transfers between devices: 74.8 us -> 0.01 us  [body(): lax.psum_scatter(picked, 'chan', scatter_dimension=0, tiled=True)]
    all_gather x1, waiting for transfers between devices: 0.01 us -> 29.4 us  [body(): gathered = lax.all_gather(small, 'chan', axis=1, tiled=True)]
    ppermute x4, waiting for transfers between devices: 70.3 us -> 76.5 us  [from_ahead(): return lax.ppermute(value, 'freq', [(q, (q - d) % n) for q in range(n)])]
  transfers between devices with their start and end apart: 6 -> 6, of which waited for: 3 -> 5; matrix products, arithmetic and copies ran while one was open for 1% -> 2% of each run, Pallas kernels for 13% -> 16%
where the time goes in v2:
time: 214 us
  waiting for transfers between devices  106 us (50%)
  Pallas kernels  62.6 us (29%)
  local copies, waits for them, and re-layouts  21.7 us (10%)
  between operations  13.7 us (6%)
  starting transfers between devices  6.6 us (3%)
    ppermute x4, waiting for transfers between devices, from_ahead(): return lax.ppermute(value, 'freq', [(q, (q - d) % n) for q in range(n)])  76.5 us
    pallas_call x3, Pallas kernels, whiten_across(): pl.pallas_call(functools.partial(whiten_kernel, count), out_shape=jax.Sha...  33.6 us
    all_gather x1, waiting for transfers between devices, body(): gathered = lax.all_gather(small, 'chan', axis=1, tiled=True)  29.4 us
    pallas_call x1, Pallas kernels, cross_lags(): pl.pallas_call(functools.partial(cross_kernel, nf, scale), out_shape=jax....  26.8 us
    unnamed x28, local copies, waits for them, and re-layouts  8.81 us
    all_gather x1, local copies, waits for them, and re-layouts, body(): gathered = lax.all_gather(small, 'chan', axis=1, tiled=True)  6.86 us
    ppermute x4, starting transfers between devices, from_ahead(): return lax.ppermute(value, 'freq', [(q, (q - d) % n) for q in range(n)])  6.56 us
    slice x1, local copies, waits for them, and re-layouts, body(): block = from_ahead(lax.slice_in_dim(records, at, at + STEP, axis=1), d)  4.77 us
  transfers between devices with their start and end apart: 6, of which 5 were waited for; matrix products, arithmetic and copies ran while one was open for 2% of the time, Pallas kernels for 16%

profile of v2, /device:TPU:0, one launch (start us, length us, event | category | flops | bytes accessed | tf_op | source)
XLA Modules:
  0.0 213.9 jit_solution(5134447574303868364)
XLA Ops:
  6.5 0.0 reduce-scatter.2.cloned.1.call-start
  6.5 0.7 and_convert_fusion
  7.2 0.7 subtract_clamp_fusion
  7.9 0.1 reshape.134
  8.0 0.1 reshape.132.owned_ref
  8.1 0.1 min.16
  8.2 0.1 min.18.row_ref
  8.3 0.0 copy-start
  8.3 2.2 %copy-done = bf16[128,32,512]{2,1,0:T(8,128)(2,1)S(1)} copy-done((bf16[128,32,512]{2,1,0:T(8,128)(2,1)S(1)}, bf16[128,32,512]{2,1,0:T(8,128)(2,1)}, u32[]{:S(2)}) %copy-start) | copy-done | bytes 4194328
  10.5 2.3 %pick.1 = bf16[128,32,512]{2,1,0:T(8,128)(2,1)S(1)} custom-call(s32[128]{0:T(128)S(1)} %reshape.132.owned_ref, s32[128]{0:T(128)S(1)} %min.18.row_ref, bf16[128,32,512]{2,1,0:T(8,128)(2,1)S(1)} %copy-done), custom_call_target="tpu_custom_call" | custom-call | tf_op jit(solution)/shard_map/pick/pallas_call | solution.py:55
  12.8 0.0 copy-start.1
  12.8 2.0 copy-done.1
  14.8 0.0 reduce-scatter.2.cloned.1.call-update
  14.9 0.0 copy-start.13
  14.9 0.0 copy-start.9
  14.9 0.0 copy-start.10
  14.9 0.0 copy-start.11
  14.9 0.0 copy-start.12
  14.9 0.0 copy-start.5
  14.9 0.0 copy-start.6
  14.9 0.0 all-gather.2.cloned.1.call-start
  15.0 4.8 %fusion.12 = (bf16[128,16,512]{2,1,0:T(8,128)(2,1)}, bf16[128,16,512]{2,1,0:T(8,128)(2,1)}) fusion(bf16[128,32,512]{2,1,0:T(8,128)(2,1)} %x_ref.3), kind=kLoop, calls=%fused_computation.37 | loop fusion | bytes 8388608 | tf_op jit(solution)/shard_map/slice | solution.py:242
  19.8 2.9 %collective-permute-start = (bf16[128,16,512]{2,1,0:T(8,128)(2,1)}, bf16[128,16,512]{2,1,0:T(8,128)(2,1)}, u32[]{:S(2)}, u32[]{:S(2)}) collective-permute-start(bf16[128,16,512]{2,1,0:T(8,128)(2,1)} %get-tuple-element.14), channel_id=1, source_target_pairs={{0,1},{1,0},{2,3},{3,2},{4,5},{5,4},{6,7},{7,6},{8,9},{9,8},{10,11... | collective-permute-start | bytes 6291464 | tf_op jit(solution)/shard_map/ppermute | solution.py:231
  22.7 0.0 collective-permute-start.1
  22.7 0.0 copy-done.13
  22.7 0.0 copy-done.9
  22.8 0.0 copy-done.10
  22.8 0.0 copy-done.11
  22.8 0.0 copy-done.12
  22.8 0.1 select_select_fusion.t_ref
  22.9 0.0 copy-done.5
  22.9 0.0 copy-done.6
  22.9 0.0 copy-start.7
  22.9 0.0 copy-start.8
  22.9 17.2 %whiten_across.3.refs_0_ = bf16[256,2,32,128]{3,2,1,0:T(8,128)(2,1)S(1)} custom-call(bf16[128,32,512]{2,1,0:T(8,128)(2,1)} %x_ref.3, f32[32,512]{1,0:T(8,128)S(1)} %select_select_fusion.t_ref, bf16[512,512]{1,0:T(8,128)(2,1)S(1)} %copy-done.5, bf16[256,256]{1,0:T(8,128)(2,1)S(1)} %copy-done.6), custom_call_target="tpu_custom_call" | custom-call | flops 4294967296 | bytes 8388608 | tf_op jit(solution)/shard_map/whiten_across/pallas_call | solution.py:100
  40.1 0.0 copy-start.2
  40.1 1.9 copy-done.2
  42.1 27.4 %collective-permute-done.x_ref = bf16[128,16,512]{2,1,0:T(8,128)(2,1)} collective-permute-done((bf16[128,16,512]{2,1,0:T(8,128)(2,1)}, bf16[128,16,512]{2,1,0:T(8,128)(2,1)}, u32[]{:S(2)}, u32[]{:S(2)}) %collective-permute-start) | collective-permute-done | bytes 2097184 | tf_op jit(solution)/shard_map/ppermute | solution.py:231
  69.5 44.0 %collective-permute-done.1.x_ref = bf16[128,16,512]{2,1,0:T(8,128)(2,1)S(1)} collective-permute-done((bf16[128,16,512]{2,1,0:T(8,128)(2,1)}, bf16[128,16,512]{2,1,0:T(8,128)(2,1)S(1)}, u32[]{:S(2)}, u32[]{:S(2)}) %collective-permute-start.1) | collective-permute-done | bytes 2097184 | tf_op jit(solution)/shard_map/ppermute | solution.py:231
  113.5 0.0 reduce-scatter.2.cloned.1.call-done
  113.5 0.0 copy-done.7
  113.5 1.3 fusion.3
  114.8 0.0 copy-done.8
  114.8 0.2 fusion.10
  115.0 0.2 multiply_convert_fusion.2
  115.3 1.8 collective-permute-start.3
  117.1 3.2 %collective-permute-done.3 = bf16[256,4,2,32]{0,3,2,1:T(8,128)(2,1)S(1)} collective-permute-done((bf16[256,4,2,32]{0,3,2,1:T(8,128)(2,1)S(1)}, bf16[256,4,2,32]{0,3,2,1:T(8,128)(2,1)S(1)}, u32[]{:S(2)}, u32[]{:S(2)}) %collective-permute-start.3) | collective-permute-done | bytes 131104 | tf_op jit(solution)/shard_map/ppermute | solution.py:231
  120.3 0.8 copy.33
  121.2 0.0 all-gather.2.cloned.1.call-update
  121.2 1.8 collective-permute-start.2
  123.0 1.8 collective-permute-done.2
  124.8 0.1 broadcast_compare_fusion.4
  124.9 0.1 select_select_fusion.1
  125.0 8.9 %whiten_across.4.refs_1_ = bf16[256,2,16,128]{3,2,1,0:T(8,128)(2,1)S(1)} custom-call(bf16[128,16,512]{2,1,0:T(8,128)(2,1)} %collective-permute-done.x_ref, f32[16,512]{1,0:T(8,128)S(1)} %get-tuple-element.20.t_ref, bf16[512,512]{1,0:T(8,128)(2,1)S(1)} %copy-done.5, bf16[256,256]{1,0:T(8,128)(2,1)S(1)} %copy-done.6), custom_call_target="tpu_custom_call" | custom-call | flops 2147483648 | bytes 4194304 | tf_op jit(solution)/shard_map/whiten_across/pallas_call | solution.py:100
  133.8 0.0 copy-start.3
  133.9 1.3 copy-done.3
  135.1 7.5 %whiten_across.5.refs_2_ = bf16[256,2,16,128]{3,2,1,0:T(8,128)(2,1)S(1)} custom-call(bf16[128,16,512]{2,1,0:T(8,128)(2,1)S(1)} %collective-permute-done.1.x_ref, f32[16,512]{1,0:T(8,128)S(1)} %get-tuple-element.19.t_ref, bf16[512,512]{1,0:T(8,128)(2,1)S(1)} %copy-done.5, bf16[256,256]{1,0:T(8,128)(2,1)S(1)} %copy-done.6), custom_call_target="tpu_custom_call" | custom-call | flops 2147483648 | bytes 4194304 | tf_op jit(solution)/shard_map/whiten_across/pallas_call | solution.py:100
  142.6 0.0 copy-start.4
  142.7 1.3 copy-done.4
  144.0 29.4 %all-gather.2.cloned.1.call-done = bf16[256,64,128]{2,0,1:T(8,128)(2,1)} async-done(((bf16[256,4,128]{2,0,1:T(8,128)(2,1)}), bf16[256,64,128]{2,0,1:T(8,128)(2,1)}) %all-gather.2.cloned.1.call-update) | async-done | bytes 4194320 | tf_op jit(solution)/shard_map/all_gather | solution.py:263
  173.4 6.9 %copy.34.refs_3_ = bf16[256,64,128]{2,1,0:T(8,128)(2,1)} copy(bf16[256,64,128]{2,0,1:T(8,128)(2,1)} %all-gather.2.cloned.1.call-done) | data formatting | bytes 8388608 | tf_op jit(solution)/shard_map/all_gather | solution.py:263
  180.3 26.8 %cross_lags.1 = bf16[128,64,256]{2,1,0:T(8,128)(2,1)} custom-call(bf16[256,2,32,128]{3,2,1,0:T(8,128)(2,1)} %copy-done.2, bf16[256,2,16,128]{3,2,1,0:T(8,128)(2,1)} %copy-done.3, bf16[256,2,16,128]{3,2,1,0:T(8,128)(2,1)} %copy-done.4, bf16[256,64,128]{2,1,0:T(8,128)(2,1)} %copy.34.refs_3_, bf16[256,512]{1,0:T(8,128)(2,1)} %constant.74.clone.refs_4_), custom_call_target="tpu_custom_call" | custom-call | tf_op jit(solution)/shard_map/cross_lags/pallas_call | solution.py:201
  (5 shorter events, 0.1 us)
Async XLA Ops:
  6.5 107.0 %reduce-scatter.2.cloned.1.call-start = ((), (), s32[]{:S(2)}) async-start(), calls=%async_computation.1 | async-start | bytes 4456448 | tf_op jit(solution)/shard_map/reduce_scatter | solution.py:251
  8.3 2.2 %copy-start = (bf16[128,32,512]{2,1,0:T(8,128)(2,1)S(1)}, bf16[128,32,512]{2,1,0:T(8,128)(2,1)}, u32[]{:S(2)}) copy-start(bf16[128,32,512]{2,1,0:T(8,128)(2,1)} %x_ref.3) | copy-start | bytes 12582916
  12.8 2.0 copy-start.1
  14.9 7.9 %copy-start.13 = (s32[32]{0:T(128)S(1)}, s32[32]{0:T(128)}, u32[]{:S(2)}) copy-start(s32[32]{0:T(128)} %param.19) | copy-start | bytes 388
  14.9 7.9 %copy-start.9 = (f32[512]{0:T(512)S(1)}, f32[512]{0:T(512)}, u32[]{:S(2)}) copy-start(f32[512]{0:T(512)} %constant.69.clone) | copy-start | bytes 6148
  14.9 7.9 %copy-start.10 = (f32[512]{0:T(512)S(1)}, f32[512]{0:T(512)}, u32[]{:S(2)}) copy-start(f32[512]{0:T(512)} %constant.68.clone) | copy-start | bytes 6148
  14.9 7.9 %copy-start.11 = (f32[512]{0:T(512)S(1)}, f32[512]{0:T(512)}, u32[]{:S(2)}) copy-start(f32[512]{0:T(512)} %constant.70.clone) | copy-start | bytes 6148
  14.9 7.9 %copy-start.12 = (f32[512]{0:T(512)S(1)}, f32[512]{0:T(512)}, u32[]{:S(2)}) copy-start(f32[512]{0:T(512)} %constant.71.clone) | copy-start | bytes 6148
  14.9 8.0 %copy-start.5 = (bf16[512,512]{1,0:T(8,128)(2,1)S(1)}, bf16[512,512]{1,0:T(8,128)(2,1)}, u32[]{:S(2)}) copy-start(bf16[512,512]{1,0:T(8,128)(2,1)} %constant.72.clone.dft_ref) | copy-start | bytes 1572868
  14.9 7.9 %copy-start.6 = (bf16[256,256]{1,0:T(8,128)(2,1)S(1)}, bf16[256,256]{1,0:T(8,128)(2,1)}, u32[]{:S(2)}) copy-start(bf16[256,256]{1,0:T(8,128)(2,1)} %constant.73.clone.band_ref) | copy-start | bytes 393220
  14.9 158.5 %all-gather.2.cloned.1.call-start = ((), (), s32[]{:S(2)}) async-start(), calls=%async_computation.2 | async-start | bytes 4456448 | tf_op jit(solution)/shard_map/all_gather | solution.py:263
  19.8 49.7 %collective-permute-start = (bf16[128,16,512]{2,1,0:T(8,128)(2,1)}, bf16[128,16,512]{2,1,0:T(8,128)(2,1)}, u32[]{:S(2)}, u32[]{:S(2)}) collective-permute-start(bf16[128,16,512]{2,1,0:T(8,128)(2,1)} %get-tuple-element.14), channel_id=1, source_target_pairs={{0,1},{1,0},{2,3},{3,2},{4,5},{5,4},{6,7},{7,6},{8,9},{9,8},{10,11... | collective-permute-start | bytes 6291464 | tf_op jit(solution)/shard_map/ppermute | solution.py:231
  22.7 90.8 %collective-permute-start.1 = (bf16[128,16,512]{2,1,0:T(8,128)(2,1)}, bf16[128,16,512]{2,1,0:T(8,128)(2,1)S(1)}, u32[]{:S(2)}, u32[]{:S(2)}) collective-permute-start(bf16[128,16,512]{2,1,0:T(8,128)(2,1)} %get-tuple-element.13), channel_id=1, source_target_pairs={{0,1},{1,0},{2,3},{3,2},{4,5},{5,4},{6,7},{7,6},{8,9},{9,8},{10,11... | collective-permute-start | bytes 6291464 | tf_op jit(solution)/shard_map/ppermute | solution.py:231
  22.9 90.6 %copy-start.7 = (bf16[512,512,1]{1,0,2:T(8,128)(2,1)S(1)}, bf16[512,512,1]{1,0,2:T(8,128)(2,1)}, u32[]{:S(2)}) copy-start(bf16[512,512,1]{1,0,2:T(8,128)(2,1)} %constant.75) | copy-start | bytes 1572868
  22.9 91.9 %copy-start.8 = (bf16[256,256,1]{1,0,2:T(8,128)(2,1)S(1)}, bf16[256,256,1]{1,0,2:T(8,128)(2,1)}, u32[]{:S(2)}) copy-start(bf16[256,256,1]{1,0,2:T(8,128)(2,1)} %constant.76) | copy-start | bytes 393220
  40.1 2.0 copy-start.2
  115.3 5.0 %collective-permute-start.3 = (bf16[256,4,2,32]{0,3,2,1:T(8,128)(2,1)S(1)}, bf16[256,4,2,32]{0,3,2,1:T(8,128)(2,1)S(1)}, u32[]{:S(2)}, u32[]{:S(2)}) collective-permute-start(bf16[256,4,2,32]{0,3,2,1:T(8,128)(2,1)S(1)} %get-tuple-element.18), channel_id=1, source_target_pairs={{0,1},{1,0},{2,3},{3,2},{4,5},{5,4},{6,7},{7,6},{8,9},{9,8},{10,11... | collective-permute-start | bytes 393224 | tf_op jit(solution)/shard_map/ppermute | solution.py:231
  121.2 3.6 %collective-permute-start.2 = (s32[32]{0:T(128)S(1)}, s32[32]{0:T(128)S(1)}, u32[]{:S(2)}, u32[]{:S(2)}) collective-permute-start(s32[32]{0:T(128)S(1)} %copy-done.13), channel_id=1, source_target_pairs={{0,1},{1,0},{2,3},{3,2},{4,5},{5,4},{6,7},{7,6},{8,9},{9,8},{10,11... | collective-permute-start | bytes 392 | tf_op jit(solution)/shard_map/ppermute | solution.py:231
  133.8 1.3 copy-start.3
  142.6 1.3 copy-start.4
Sparse Core Ops, SparseCore 0:
  15.0 75.2 reduce-scatter.1
  121.3 52.0 all-gather.1

commit v3 on v2

--- a/solution.py
+++ b/solution.py
@@ -243,16 +243,29 @@
             arrived.append((block, select[at : at + STEP]))
 
     index = jnp.pad(source_index.reshape(n, per), ((0, 0), (0, share * m - per)), constant_values=-1)
-    index = index.reshape(n, m, share).transpose(1, 0, 2).reshape(-1)
-    rows = index - mine * chans
-    owned = (rows >= 0) & (rows < chans) & (index >= 0)
-    rows = jnp.clip(rows, 0, chans - 1)
-    picked = pick(records, owned.astype(jnp.int32), rows.astype(jnp.int32))
-    own_sources = lax.psum_scatter(picked, "chan", scatter_dimension=0, tiled=True)
+    index = index.reshape(n, 2, m // 2, share).transpose(1, 2, 0, 3).reshape(2, -1)
+    side = lax.rem(mine, 2)
+    groups = [list(range(c, m, 2)) for c in range(2)]
+    swap = [(q, q ^ 1) for q in range(m)]
+
+    def pick_for(index):
+        rows = index - mine * chans
+        owned = (rows >= 0) & (rows < chans) & (index >= 0)
+        rows = jnp.clip(rows, 0, chans - 1)
+        return pick(records, owned.astype(jnp.int32), rows.astype(jnp.int32))
+
+    given = pick_for(jnp.where(side == 0, index[1], index[0]))
+    given = lax.ppermute(given, "chan", swap)
+    picked = pick_for(jnp.where(side == 0, index[0], index[1])) + given
+    own_sources = lax.psum_scatter(
+        picked, "chan", scatter_dimension=0, axis_index_groups=groups, tiled=True
+    )
     own_taper = taper_of(taper_select)
     receivers = [whiten_across(records, own_taper, dft, band, count)]
     blocks = [block for block, _ in arrived]
-    own_sources, receivers, blocks = lax.optimization_barrier((own_sources, receivers, blocks))
+    early = blocks[: len(blocks) // 2]
+    own_sources, receivers, early = lax.optimization_barrier((own_sources, receivers, early))
+    blocks = early + blocks[len(blocks) // 2 :]
     spectra = whiten_rows(own_sources, own_taper[None], dft, band, count)
     spectra = spectra.reshape(n, share, segs, 2, nfreq).transpose(0, 4, 1, 3, 2)
     pieces = []
@@ -260,8 +273,11 @@
         give = lax.dynamic_index_in_dim(spectra, (me - d) % n, 0, keepdims=False)
         pieces.append(from_ahead(give, d) if d else give)
     small = jnp.stack(pieces, axis=3).reshape(nfreq, share, 2 * n * segs)
-    gathered = lax.all_gather(small, "chan", axis=1, tiled=True)
-    sources = gathered[:, :per]
+    gathered = lax.all_gather(small, "chan", axis=1, axis_index_groups=groups, tiled=True)
+    other = lax.ppermute(gathered, "chan", swap)
+    first = jnp.where(side == 0, gathered, other)
+    second = jnp.where(side == 0, other, gathered)
+    sources = jnp.concatenate([first, second], axis=1)[:, :per]
 
     for block, (_, select) in zip(blocks, arrived):
         receivers.append(whiten_across(block, taper_of(select), dft, band, count))

time: 214 us -> 210 us (0.981)
  waiting for transfers between devices: 106 us -> 96.6 us
  other arithmetic: 1.62 us -> 9.04 us
  local copies, waits for them, and re-layouts: 21.7 us -> 17.5 us
    ppermute x4, waiting for transfers between devices: 76.5 us -> 32.7 us  [from_ahead(): return lax.ppermute(value, 'freq', [(q, (q - d) % n) for q in range(n)])]
    all_gather x1, waiting for transfers between devices: 29.4 us -> 47 us  [body(): lax.all_gather(small, 'chan', axis=1, axis_index_groups=groups, tiled=True)]
    reduce_scatter x1, waiting for transfers between devices: 0.01 us -> 16.8 us  [body(): lax.psum_scatter(picked, 'chan', scatter_dimension=0, axis_index_groups=g...]
    all_gather x1, local copies, waits for them, and re-layouts: 6.86 us -> 2.94 us  [body(): lax.all_gather(small, 'chan', axis=1, axis_index_groups=groups, tiled=True)]
    add x0 -> x1, other arithmetic: none -> 3.91 us  [body(): picked = pick_for(jnp.where(side == 0, index[0], index[1])) + given]
    concatenate x0 -> x1, other arithmetic: none -> 3.52 us  [body(): sources = jnp.concatenate([first, second], axis=1)[:, :per]]
    unnamed x28 -> x30, local copies, waits for them, and re-layouts: 8.81 us -> 7.78 us
  transfers between devices with their start and end apart: 6 -> 8, of which waited for: 5 -> 6; matrix products, arithmetic and copies ran while one was open for 2% -> 4% of each run, Pallas kernels for 16% -> 17%
where the time goes in v3:
time: 210 us; the launch traced here: 209 us
  waiting for transfers between devices  96.6 us (46%)
  Pallas kernels  63.1 us (30%)
  local copies, waits for them, and re-layouts  17.5 us (8%)
  between operations  13.8 us (7%)
  other arithmetic  9.04 us (4%)
  starting transfers between devices  7.51 us (4%)
    all_gather x1, waiting for transfers between devices, body(): lax.all_gather(small, 'chan', axis=1, axis_index_groups=groups, tiled=True)  47 us
    pallas_call x3, Pallas kernels, whiten_across(): pl.pallas_call(functools.partial(whiten_kernel, count), out_shape=jax.Sha...  33.5 us
    ppermute x4, waiting for transfers between devices, from_ahead(): return lax.ppermute(value, 'freq', [(q, (q - d) % n) for q in range(n)])  32.7 us
    pallas_call x1, Pallas kernels, cross_lags(): pl.pallas_call(functools.partial(cross_kernel, nf, scale), out_shape=jax....  26.8 us
    reduce_scatter x1, waiting for transfers between devices, body(): lax.psum_scatter(picked, 'chan', scatter_dimension=0, axis_index_groups=g...  16.8 us
    unnamed x30, local copies, waits for them, and re-layouts  7.78 us
    ppermute x4, starting transfers between devices, from_ahead(): return lax.ppermute(value, 'freq', [(q, (q - d) % n) for q in range(n)])  6.88 us
    slice x1, local copies, waits for them, and re-layouts, body(): block = from_ahead(lax.slice_in_dim(records, at, at + STEP, axis=1), d)  4.84 us
  transfers between devices with their start and end apart: 8, of which 6 were waited for; matrix products, arithmetic and copies ran while one was open for 4% of the time, Pallas kernels for 17%

profile of v3, /device:TPU:0, one launch (start us, length us, event | category | flops | bytes accessed | tf_op | source)
XLA Modules:
  0.0 209.3 jit_solution(10553707924842836555)
XLA Ops:
  6.5 0.0 reduce-scatter.2.cloned.1.call-start
  6.5 0.7 reshape.140
  7.3 0.1 min.20.row_ref
  7.5 0.1 reshape.145.owned_ref
  7.5 0.0 copy-start
  7.6 2.2 %copy-done = bf16[128,32,512]{2,1,0:T(8,128)(2,1)S(1)} copy-done((bf16[128,32,512]{2,1,0:T(8,128)(2,1)S(1)}, bf16[128,32,512]{2,1,0:T(8,128)(2,1)}, u32[]{:S(2)}) %copy-start) | copy-done | bytes 4194328
  9.7 1.4 pick.3
  11.2 0.5 collective-permute-start
  11.7 0.1 reshape.144.owned_ref
  11.8 0.1 min.18.row_ref
  11.9 0.0 copy-start.1
  11.9 2.2 %copy-done.1 = bf16[128,32,512]{2,1,0:T(8,128)(2,1)S(1)} copy-done((bf16[128,32,512]{2,1,0:T(8,128)(2,1)S(1)}, bf16[128,32,512]{2,1,0:T(8,128)(2,1)}, u32[]{:S(2)}) %copy-start.1) | copy-done | bytes 4194328
  14.1 1.4 pick.2
  15.5 0.1 collective-permute-done
  15.6 3.9 %add.32 = bf16[64,32,512]{2,1,0:T(8,128)(2,1)} add(bf16[64,32,512]{2,1,0:T(8,128)(2,1)S(1)} %pick.2, bf16[64,32,512]{2,1,0:T(8,128)(2,1)} %collective-permute-done) | non-fusion elementwise | flops 1048576 | bytes 6291456 | tf_op jit(solution)/shard_map/add | solution.py:259
  19.5 0.0 reduce-scatter.2.cloned.1.call-update
  19.5 0.0 copy-start.14
  19.5 0.0 copy-start.10
  19.6 0.0 copy-start.11
  19.6 0.0 copy-start.12
  19.6 0.0 copy-start.13
  19.6 0.0 copy-start.5
  19.6 0.0 copy-start.6
  19.6 0.0 all-gather.2.cloned.1.call-start
  19.7 4.8 %fusion.12 = (bf16[128,16,512]{2,1,0:T(8,128)(2,1)}, bf16[128,16,512]{2,1,0:T(8,128)(2,1)}) fusion(bf16[128,32,512]{2,1,0:T(8,128)(2,1)} %x_ref.5), kind=kLoop, calls=%fused_computation.44 | loop fusion | bytes 8388608 | tf_op jit(solution)/shard_map/slice | solution.py:242
  24.5 2.9 %collective-permute-start.1 = (bf16[128,16,512]{2,1,0:T(8,128)(2,1)}, bf16[128,16,512]{2,1,0:T(8,128)(2,1)S(1)}, u32[]{:S(2)}, u32[]{:S(2)}) collective-permute-start(bf16[128,16,512]{2,1,0:T(8,128)(2,1)} %get-tuple-element.14), channel_id=1, source_target_pairs={{0,1},{1,0},{2,3},{3,2},{4,5},{5,4},{6,7},{7,6},{8,9},{9,8},{10,11... | collective-permute-start | bytes 6291464 | tf_op jit(solution)/shard_map/ppermute | solution.py:231
  27.4 0.0 copy-done.14
  27.4 0.0 copy-done.10
  27.4 0.0 copy-done.11
  27.4 0.0 copy-done.12
  27.4 0.0 copy-done.13
  27.4 0.1 select_select_fusion.t_ref
  27.5 0.0 copy-start.8
  27.5 0.0 copy-start.9
  27.6 17.2 %whiten_across.3.refs_0_ = bf16[256,2,32,128]{3,2,1,0:T(8,128)(2,1)S(1)} custom-call(bf16[128,32,512]{2,1,0:T(8,128)(2,1)} %x_ref.5, f32[32,512]{1,0:T(8,128)S(1)} %select_select_fusion.t_ref, bf16[512,512]{1,0:T(8,128)(2,1)S(1)} %copy-done.5, bf16[256,256]{1,0:T(8,128)(2,1)S(1)} %copy-done.6), custom_call_target="tpu_custom_call" | custom-call | flops 4294967296 | bytes 8388608 | tf_op jit(solution)/shard_map/whiten_across/pallas_call | solution.py:100
  44.7 0.0 copy-start.2
  44.8 1.9 copy-done.2
  46.7 26.8 %collective-permute-done.1.x_ref = bf16[128,16,512]{2,1,0:T(8,128)(2,1)S(1)} collective-permute-done((bf16[128,16,512]{2,1,0:T(8,128)(2,1)}, bf16[128,16,512]{2,1,0:T(8,128)(2,1)S(1)}, u32[]{:S(2)}, u32[]{:S(2)}) %collective-permute-start.1) | collective-permute-done | bytes 2097184 | tf_op jit(solution)/shard_map/ppermute | solution.py:231
  73.5 16.8 %reduce-scatter.2.cloned.1.call-done = bf16[8,32,512]{2,1,0:T(8,128)(2,1)} async-done(((bf16[64,32,512]{2,1,0:T(8,128)(2,1)}), bf16[8,32,512]{2,1,0:T(8,128)(2,1)}) %reduce-scatter.2.cloned.1.call-update) | async-done | bytes 262160 | tf_op jit(solution)/shard_map/reduce_scatter | solution.py:260
  90.3 1.3 fusion.3
  91.6 0.2 fusion.10
  91.8 0.2 multiply_convert_fusion.2
  92.1 1.2 collective-permute-start.4
  93.3 3.8 %collective-permute-done.4 = bf16[256,4,2,32]{0,3,2,1:T(8,128)(2,1)S(1)} collective-permute-done((bf16[256,4,2,32]{0,3,2,1:T(8,128)(2,1)S(1)}, bf16[256,4,2,32]{0,3,2,1:T(8,128)(2,1)S(1)}, u32[]{:S(2)}, u32[]{:S(2)}) %collective-permute-start.4) | collective-permute-done | bytes 131104 | tf_op jit(solution)/shard_map/ppermute | solution.py:231
  97.2 0.9 copy.39
  98.0 0.0 all-gather.2.cloned.1.call-update
  98.0 1.2 collective-permute-start.3
  99.3 47.0 %all-gather.2.cloned.1.call-done = bf16[256,32,128]{2,0,1:T(8,128)(2,1)} async-done(((bf16[256,4,128]{2,0,1:T(8,128)(2,1)}), bf16[256,32,128]{2,0,1:T(8,128)(2,1)}) %all-gather.2.cloned.1.call-update) | async-done | bytes 2097168 | tf_op jit(solution)/shard_map/all_gather | solution.py:276
  146.3 2.9 %copy.41 = bf16[256,32,128]{2,1,0:T(8,128)(2,1)S(1)} copy(bf16[256,32,128]{2,0,1:T(8,128)(2,1)} %all-gather.2.cloned.1.call-done) | data formatting | bytes 4194304 | tf_op jit(solution)/shard_map/all_gather | solution.py:276
  149.2 0.1 collective-permute-start.5
  149.3 1.5 collective-permute-start.2
  150.8 2.1 collective-permute-done.2
  152.9 0.1 broadcast_compare_fusion.4
  153.0 0.1 select_select_fusion.1
  153.1 0.0 collective-permute-done.3.x_ref
  153.1 8.9 %whiten_across.5.refs_2_ = bf16[256,2,16,128]{3,2,1,0:T(8,128)(2,1)S(1)} custom-call(bf16[128,16,512]{2,1,0:T(8,128)(2,1)} %collective-permute-done.3.x_ref, f32[16,512]{1,0:T(8,128)S(1)} %get-tuple-element.23.t_ref, bf16[512,512]{1,0:T(8,128)(2,1)S(1)} %copy-done.5, bf16[256,256]{1,0:T(8,128)(2,1)S(1)} %copy-done.6), custom_call_target="tpu_custom_call" | custom-call | flops 2147483648 | bytes 4194304 | tf_op jit(solution)/shard_map/whiten_across/pallas_call | solution.py:100
  162.0 1.4 copy-done.3
  163.3 7.5 %whiten_across.4.refs_1_ = bf16[256,2,16,128]{3,2,1,0:T(8,128)(2,1)S(1)} custom-call(bf16[128,16,512]{2,1,0:T(8,128)(2,1)S(1)} %collective-permute-done.1.x_ref, f32[16,512]{1,0:T(8,128)S(1)} %get-tuple-element.24.t_ref, bf16[512,512]{1,0:T(8,128)(2,1)S(1)} %copy-done.5, bf16[256,256]{1,0:T(8,128)(2,1)S(1)} %copy-done.6), custom_call_target="tpu_custom_call" | custom-call | flops 2147483648 | bytes 4194304 | tf_op jit(solution)/shard_map/whiten_across/pallas_call | solution.py:100
  170.8 0.0 collective-permute-done.5
  170.8 0.0 copy-done.7
  170.8 1.3 broadcast_select_fusion.1
  172.1 0.0 copy-done.4
  172.2 3.5 %pad_maximum_fusion.refs_3_ = bf16[256,64,128]{2,1,0:T(8,128)(2,1)} fusion(bf16[256,32,128]{2,1,0:T(8,128)(2,1)S(1)} %get-tuple-element.12, bf16[256,32,128]{2,1,0:T(8,128)(2,1)S(1)} %get-tuple-element.11), kind=kLoop, calls=%fused_computation | loop fusion | flops 8388608 | bytes 8388608 | tf_op jit(solution)/shard_map/concatenate | solution.py:280
  175.7 26.8 %cross_lags.1 = bf16[128,64,256]{2,1,0:T(8,128)(2,1)} custom-call(bf16[256,2,32,128]{3,2,1,0:T(8,128)(2,1)} %copy-done.2, bf16[256,2,16,128]{3,2,1,0:T(8,128)(2,1)} %copy-done.4, bf16[256,2,16,128]{3,2,1,0:T(8,128)(2,1)} %copy-done.3, bf16[256,64,128]{2,1,0:T(8,128)(2,1)} %pad_maximum_fusion.refs_3_, bf16[256,512]{1,0:T(8,128)(2,1)} %constant.76.clone.refs_4_), custom_call_target="tpu_custom_call" | custom-call | tf_op jit(solution)/shard_map/cross_lags/pallas_call | solution.py:201
  (16 shorter events, 0.1 us)
Async XLA Ops:
  6.5 83.8 %reduce-scatter.2.cloned.1.call-start = ((), (), s32[]{:S(2)}) async-start(), calls=%async_computation.1 | async-start | bytes 2359296 | tf_op jit(solution)/shard_map/reduce_scatter | solution.py:260
  7.5 2.2 %copy-start = (bf16[128,32,512]{2,1,0:T(8,128)(2,1)S(1)}, bf16[128,32,512]{2,1,0:T(8,128)(2,1)}, u32[]{:S(2)}) copy-start(bf16[128,32,512]{2,1,0:T(8,128)(2,1)} %x_ref.5) | copy-start | bytes 12582916
  11.2 4.4 %collective-permute-start = (bf16[64,32,512]{2,1,0:T(8,128)(2,1)S(1)}, bf16[64,32,512]{2,1,0:T(8,128)(2,1)}, u32[]{:S(2)}, u32[]{:S(2)}) collective-permute-start(bf16[64,32,512]{2,1,0:T(8,128)(2,1)S(1)} %pick.3), channel_id=1, source_target_pairs={{0,2},{2,0},{4,6},{6,4},{8,10},{10,8},{12,14},{14,12},{16,18},{18,... | collective-permute-start | bytes 6291464 | tf_op jit(solution)/shard_map/ppermute | solution.py:258
  11.9 2.2 %copy-start.1 = (bf16[128,32,512]{2,1,0:T(8,128)(2,1)S(1)}, bf16[128,32,512]{2,1,0:T(8,128)(2,1)}, u32[]{:S(2)}) copy-start(bf16[128,32,512]{2,1,0:T(8,128)(2,1)} %x_ref.5) | copy-start | bytes 12582916
  19.5 7.8 %copy-start.14 = (s32[32]{0:T(128)S(1)}, s32[32]{0:T(128)}, u32[]{:S(2)}) copy-start(s32[32]{0:T(128)} %param.19) | copy-start | bytes 388
  19.5 7.8 %copy-start.10 = (f32[512]{0:T(512)S(1)}, f32[512]{0:T(512)}, u32[]{:S(2)}) copy-start(f32[512]{0:T(512)} %constant.73.clone) | copy-start | bytes 6148
  19.6 7.8 %copy-start.11 = (f32[512]{0:T(512)S(1)}, f32[512]{0:T(512)}, u32[]{:S(2)}) copy-start(f32[512]{0:T(512)} %constant.72.clone) | copy-start | bytes 6148
  19.6 7.8 %copy-start.12 = (f32[512]{0:T(512)S(1)}, f32[512]{0:T(512)}, u32[]{:S(2)}) copy-start(f32[512]{0:T(512)} %constant.71.clone) | copy-start | bytes 6148
  19.6 7.8 %copy-start.13 = (f32[512]{0:T(512)S(1)}, f32[512]{0:T(512)}, u32[]{:S(2)}) copy-start(f32[512]{0:T(512)} %constant.70.clone) | copy-start | bytes 6148
  19.6 7.9 %copy-start.5 = (bf16[512,512]{1,0:T(8,128)(2,1)S(1)}, bf16[512,512]{1,0:T(8,128)(2,1)}, u32[]{:S(2)}) copy-start(bf16[512,512]{1,0:T(8,128)(2,1)} %constant.74.clone.dft_ref) | copy-start | bytes 1572868
  19.6 7.9 %copy-start.6 = (bf16[256,256]{1,0:T(8,128)(2,1)S(1)}, bf16[256,256]{1,0:T(8,128)(2,1)}, u32[]{:S(2)}) copy-start(bf16[256,256]{1,0:T(8,128)(2,1)} %constant.75.clone.band_ref) | copy-start | bytes 393220
  19.6 126.7 %all-gather.2.cloned.1.call-start = ((), (), s32[]{:S(2)}) async-start(), calls=%async_computation.2 | async-start | bytes 2359296 | tf_op jit(solution)/shard_map/all_gather | solution.py:276
  24.5 49.0 %collective-permute-start.1 = (bf16[128,16,512]{2,1,0:T(8,128)(2,1)}, bf16[128,16,512]{2,1,0:T(8,128)(2,1)S(1)}, u32[]{:S(2)}, u32[]{:S(2)}) collective-permute-start(bf16[128,16,512]{2,1,0:T(8,128)(2,1)} %get-tuple-element.14), channel_id=1, source_target_pairs={{0,1},{1,0},{2,3},{3,2},{4,5},{5,4},{6,7},{7,6},{8,9},{9,8},{10,11... | collective-permute-start | bytes 6291464 | tf_op jit(solution)/shard_map/ppermute | solution.py:231
  27.5 62.8 %copy-start.8 = (bf16[512,512,1]{1,0,2:T(8,128)(2,1)S(1)}, bf16[512,512,1]{1,0,2:T(8,128)(2,1)}, u32[]{:S(2)}) copy-start(bf16[512,512,1]{1,0,2:T(8,128)(2,1)} %constant.77) | copy-start | bytes 1572868
  27.5 64.1 %copy-start.9 = (bf16[256,256,1]{1,0,2:T(8,128)(2,1)S(1)}, bf16[256,256,1]{1,0,2:T(8,128)(2,1)}, u32[]{:S(2)}) copy-start(bf16[256,256,1]{1,0,2:T(8,128)(2,1)} %constant.78) | copy-start | bytes 393220
  44.7 2.0 copy-start.2
  92.1 5.0 %collective-permute-start.4 = (bf16[256,4,2,32]{0,3,2,1:T(8,128)(2,1)S(1)}, bf16[256,4,2,32]{0,3,2,1:T(8,128)(2,1)S(1)}, u32[]{:S(2)}, u32[]{:S(2)}) collective-permute-start(bf16[256,4,2,32]{0,3,2,1:T(8,128)(2,1)S(1)} %get-tuple-element.18), channel_id=1, source_target_pairs={{0,1},{1,0},{2,3},{3,2},{4,5},{5,4},{6,7},{7,6},{8,9},{9,8},{10,11... | collective-permute-start | bytes 393224 | tf_op jit(solution)/shard_map/ppermute | solution.py:231
  98.0 55.0 %collective-permute-start.3 = (bf16[128,16,512]{2,1,0:T(8,128)(2,1)}, bf16[128,16,512]{2,1,0:T(8,128)(2,1)}, u32[]{:S(2)}, u32[]{:S(2)}) collective-permute-start(bf16[128,16,512]{2,1,0:T(8,128)(2,1)} %get-tuple-element.13), channel_id=1, source_target_pairs={{0,1},{1,0},{2,3},{3,2},{4,5},{5,4},{6,7},{7,6},{8,9},{9,8},{10,11... | collective-permute-start | bytes 6291464 | tf_op jit(solution)/shard_map/ppermute | solution.py:231
  149.2 21.6 %collective-permute-start.5 = (bf16[256,32,128]{2,1,0:T(8,128)(2,1)S(1)}, bf16[256,32,128]{2,1,0:T(8,128)(2,1)S(1)}, u32[]{:S(2)}, u32[]{:S(2)}) collective-permute-start(bf16[256,32,128]{2,1,0:T(8,128)(2,1)S(1)} %copy.41), channel_id=1, source_target_pairs={{0,2},{2,0},{4,6},{6,4},{8,10},{10,8},{12,14},{14,12},{16,18},{18,... | collective-permute-start | bytes 6291464 | tf_op jit(solution)/shard_map/ppermute | solution.py:277
  149.3 3.6 %collective-permute-start.2 = (s32[32]{0:T(128)S(1)}, s32[32]{0:T(128)S(1)}, u32[]{:S(2)}, u32[]{:S(2)}) collective-permute-start(s32[32]{0:T(128)S(1)} %copy-done.14), channel_id=1, source_target_pairs={{0,1},{1,0},{2,3},{3,2},{4,5},{5,4},{6,7},{7,6},{8,9},{9,8},{10,11... | collective-permute-start | bytes 392 | tf_op jit(solution)/shard_map/ppermute | solution.py:231
  162.0 1.4 copy-start.3
  163.3 7.5 %copy-start.7 = (bf16[256,32,128]{2,0,1:T(8,128)(2,1)S(1)}, bf16[256,32,128]{2,0,1:T(8,128)(2,1)}, u32[]{:S(2)}) copy-start(bf16[256,32,128]{2,0,1:T(8,128)(2,1)} %all-gather.2.cloned.1.call-done) | copy-start | bytes 6291460
  170.8 1.4 copy-start.4
Sparse Core Ops, SparseCore 0:
  19.7 70.6 reduce-scatter.1
  98.2 48.0 all-gather.1

commit v4 on v3

--- a/solution.py
+++ b/solution.py
@@ -274,13 +274,14 @@
         pieces.append(from_ahead(give, d) if d else give)
     small = jnp.stack(pieces, axis=3).reshape(nfreq, share, 2 * n * segs)
     gathered = lax.all_gather(small, "chan", axis=1, axis_index_groups=groups, tiled=True)
+    for block, (_, select) in zip(blocks, arrived):
+        receivers.append(whiten_across(block, taper_of(select), dft, band, count))
+    gathered, receivers = lax.optimization_barrier((gathered, receivers))
     other = lax.ppermute(gathered, "chan", swap)
     first = jnp.where(side == 0, gathered, other)
     second = jnp.where(side == 0, other, gathered)
     sources = jnp.concatenate([first, second], axis=1)[:, :per]
 
-    for block, (_, select) in zip(blocks, arrived):
-        receivers.append(whiten_across(block, taper_of(select), dft, band, count))
     return cross_lags(receivers, sources, inverse, 1.0 / math.sqrt(n * segs))
 
 

time: 210 us -> 207 us (0.986)
    all_gather x1, waiting for transfers between devices: 47 us -> 0.01 us  [body(): lax.all_gather(small, 'chan', axis=1, axis_index_groups=groups, tiled=True)]
    ppermute x4, waiting for transfers between devices: 32.7 us -> 73.5 us  [from_ahead(): return lax.ppermute(value, 'freq', [(q, (q - d) % n) for q in range(n)])]
    ppermute x1, waiting for transfers between devices: 0.01 us -> 4.15 us  [body(): other = lax.ppermute(gathered, 'chan', swap)]
    optimization_barrier x0 -> x1, local copies, waits for them, and re-layouts: none -> 3.09 us  [body(): gathered, receivers = lax.optimization_barrier((gathered, receivers))]
    all_gather x1 -> x0, local copies, waits for them, and re-layouts: 2.94 us -> none  [body(): lax.all_gather(small, 'chan', axis=1, axis_index_groups=groups, tiled=True)]
  transfers between devices with their start and end apart: 8 -> 8, of which waited for: 6 -> 6; matrix products, arithmetic and copies ran while one was open for 4% -> 3% of each run, Pallas kernels for 17% -> 16%
where the time goes in v4:
time: 207 us; the launch traced here: 206 us
  waiting for transfers between devices  94.6 us (46%)
  Pallas kernels  61.5 us (30%)
  local copies, waits for them, and re-layouts  19 us (9%)
  between operations  13.7 us (7%)
  other arithmetic  9.11 us (4%)
  starting transfers between devices  6.83 us (3%)
    ppermute x4, waiting for transfers between devices, from_ahead(): return lax.ppermute(value, 'freq', [(q, (q - d) % n) for q in range(n)])  73.5 us
    pallas_call x3, Pallas kernels, whiten_across(): pl.pallas_call(functools.partial(whiten_kernel, count), out_shape=jax.Sha...  31.9 us
    pallas_call x1, Pallas kernels, cross_lags(): pl.pallas_call(functools.partial(cross_kernel, nf, scale), out_shape=jax....  26.8 us
    reduce_scatter x1, waiting for transfers between devices, body(): lax.psum_scatter(picked, 'chan', scatter_dimension=0, axis_index_groups=g...  16.8 us
    unnamed x30, local copies, waits for them, and re-layouts  9.09 us
    ppermute x4, starting transfers between devices, from_ahead(): return lax.ppermute(value, 'freq', [(q, (q - d) % n) for q in range(n)])  6.19 us
    slice x1, local copies, waits for them, and re-layouts, body(): block = from_ahead(lax.slice_in_dim(records, at, at + STEP, axis=1), d)  4.84 us
    ppermute x1, waiting for transfers between devices, body(): other = lax.ppermute(gathered, 'chan', swap)  4.15 us
  transfers between devices with their start and end apart: 8, of which 6 were waited for; matrix products, arithmetic and copies ran while one was open for 3% of the time, Pallas kernels for 16%

profile of v4, /device:TPU:0, one launch (start us, length us, event | category | flops | bytes accessed | tf_op | source)
XLA Modules:
  0.0 206.5 jit_solution(10646446713252453790)
XLA Ops:
  6.5 0.0 reduce-scatter.2.cloned.1.call-start
  6.5 0.7 reshape.140
  7.3 0.1 min.20.row_ref
  7.5 0.1 reshape.145.owned_ref
  7.5 0.0 copy-start
  7.6 2.2 %copy-done = bf16[128,32,512]{2,1,0:T(8,128)(2,1)S(1)} copy-done((bf16[128,32,512]{2,1,0:T(8,128)(2,1)S(1)}, bf16[128,32,512]{2,1,0:T(8,128)(2,1)}, u32[]{:S(2)}) %copy-start) | copy-done | bytes 4194328
  9.7 1.4 pick.3
  11.2 0.5 collective-permute-start
  11.7 0.1 reshape.144.owned_ref
  11.8 0.1 min.18.row_ref
  11.9 0.0 copy-start.1
  11.9 2.2 %copy-done.1 = bf16[128,32,512]{2,1,0:T(8,128)(2,1)S(1)} copy-done((bf16[128,32,512]{2,1,0:T(8,128)(2,1)S(1)}, bf16[128,32,512]{2,1,0:T(8,128)(2,1)}, u32[]{:S(2)}) %copy-start.1) | copy-done | bytes 4194328
  14.1 1.4 pick.2
  15.5 0.1 collective-permute-done
  15.6 3.9 %add.32 = bf16[64,32,512]{2,1,0:T(8,128)(2,1)} add(bf16[64,32,512]{2,1,0:T(8,128)(2,1)S(1)} %pick.2, bf16[64,32,512]{2,1,0:T(8,128)(2,1)} %collective-permute-done) | non-fusion elementwise | flops 1048576 | bytes 6291456 | tf_op jit(solution)/shard_map/add | solution.py:259
  19.5 0.0 reduce-scatter.2.cloned.1.call-update
  19.5 0.0 copy-start.14
  19.5 0.0 copy-start.10
  19.6 0.0 copy-start.11
  19.6 0.0 copy-start.12
  19.6 0.0 copy-start.13
  19.6 0.0 copy-start.5
  19.6 0.0 copy-start.6
  19.6 0.0 all-gather.2.cloned.1.call-start
  19.7 4.8 %fusion.12 = (bf16[128,16,512]{2,1,0:T(8,128)(2,1)}, bf16[128,16,512]{2,1,0:T(8,128)(2,1)}) fusion(bf16[128,32,512]{2,1,0:T(8,128)(2,1)} %x_ref.5), kind=kLoop, calls=%fused_computation.44 | loop fusion | bytes 8388608 | tf_op jit(solution)/shard_map/slice | solution.py:242
  24.5 2.9 %collective-permute-start.1 = (bf16[128,16,512]{2,1,0:T(8,128)(2,1)}, bf16[128,16,512]{2,1,0:T(8,128)(2,1)S(1)}, u32[]{:S(2)}, u32[]{:S(2)}) collective-permute-start(bf16[128,16,512]{2,1,0:T(8,128)(2,1)} %get-tuple-element.22), channel_id=1, source_target_pairs={{0,1},{1,0},{2,3},{3,2},{4,5},{5,4},{6,7},{7,6},{8,9},{9,8},{10,11... | collective-permute-start | bytes 6291464 | tf_op jit(solution)/shard_map/ppermute | solution.py:231
  27.4 0.0 copy-done.14
  27.4 0.0 copy-done.10
  27.4 0.0 copy-done.11
  27.4 0.0 copy-done.12
  27.4 0.0 copy-done.13
  27.4 0.1 select_select_fusion.t_ref
  27.5 0.0 copy-done.5
  27.5 0.0 copy-done.6
  27.5 0.0 copy-start.8
  27.5 0.0 copy-start.9
  27.6 17.2 %whiten_across.3.refs_0_ = bf16[256,2,32,128]{3,2,1,0:T(8,128)(2,1)S(1)} custom-call(bf16[128,32,512]{2,1,0:T(8,128)(2,1)} %x_ref.5, f32[32,512]{1,0:T(8,128)S(1)} %select_select_fusion.t_ref, bf16[512,512]{1,0:T(8,128)(2,1)S(1)} %copy-done.5, bf16[256,256]{1,0:T(8,128)(2,1)S(1)} %copy-done.6), custom_call_target="tpu_custom_call" | custom-call | flops 4294967296 | bytes 8388608 | tf_op jit(solution)/shard_map/whiten_across/pallas_call | solution.py:100
  44.8 1.9 copy-done.2
  46.7 26.8 %collective-permute-done.1.x_ref = bf16[128,16,512]{2,1,0:T(8,128)(2,1)S(1)} collective-permute-done((bf16[128,16,512]{2,1,0:T(8,128)(2,1)}, bf16[128,16,512]{2,1,0:T(8,128)(2,1)S(1)}, u32[]{:S(2)}, u32[]{:S(2)}) %collective-permute-start.1) | collective-permute-done | bytes 2097184 | tf_op jit(solution)/shard_map/ppermute | solution.py:231
  73.5 16.8 %reduce-scatter.2.cloned.1.call-done = bf16[8,32,512]{2,1,0:T(8,128)(2,1)} async-done(((bf16[64,32,512]{2,1,0:T(8,128)(2,1)}), bf16[8,32,512]{2,1,0:T(8,128)(2,1)}) %reduce-scatter.2.cloned.1.call-update) | async-done | bytes 262160 | tf_op jit(solution)/shard_map/reduce_scatter | solution.py:260
  90.3 1.3 fusion.3
  91.6 0.0 copy-done.9
  91.6 0.2 fusion.10
  91.8 0.2 multiply_convert_fusion.2
  92.1 1.2 collective-permute-start.2
  93.3 3.8 %collective-permute-done.2 = bf16[256,4,2,32]{0,3,2,1:T(8,128)(2,1)S(1)} collective-permute-done((bf16[256,4,2,32]{0,3,2,1:T(8,128)(2,1)S(1)}, bf16[256,4,2,32]{0,3,2,1:T(8,128)(2,1)S(1)}, u32[]{:S(2)}, u32[]{:S(2)}) %collective-permute-start.2) | collective-permute-done | bytes 131104 | tf_op jit(solution)/shard_map/ppermute | solution.py:231
  97.2 0.9 copy.39
  98.0 0.0 all-gather.2.cloned.1.call-update
  98.0 1.2 collective-permute-start.4
  99.3 0.8 collective-permute-start.3
  100.1 42.9 %collective-permute-done.3 = s32[32]{0:T(128)S(1)} collective-permute-done((s32[32]{0:T(128)S(1)}, s32[32]{0:T(128)S(1)}, u32[]{:S(2)}, u32[]{:S(2)}) %collective-permute-start.3) | collective-permute-done | bytes 160 | tf_op jit(solution)/shard_map/ppermute | solution.py:231
  143.0 0.1 broadcast_compare_fusion.4
  143.1 0.1 select_select_fusion.1
  143.2 0.0 collective-permute-done.4.x_ref
  143.2 7.3 %whiten_across.5.refs_2_ = bf16[256,2,16,128]{3,2,1,0:T(8,128)(2,1)S(1)} custom-call(bf16[128,16,512]{2,1,0:T(8,128)(2,1)S(1)} %collective-permute-done.4.x_ref, f32[16,512]{1,0:T(8,128)S(1)} %get-tuple-element.31.t_ref, bf16[512,512]{1,0:T(8,128)(2,1)S(1)} %copy-done.5, bf16[256,256]{1,0:T(8,128)(2,1)S(1)} %copy-done.6), custom_call_target="tpu_custom_call" | custom-call | flops 2147483648 | bytes 4194304 | tf_op jit(solution)/shard_map/whiten_across/pallas_call | solution.py:100
  150.5 1.4 copy-done.3
  151.8 7.5 %whiten_across.4.refs_1_ = bf16[256,2,16,128]{3,2,1,0:T(8,128)(2,1)S(1)} custom-call(bf16[128,16,512]{2,1,0:T(8,128)(2,1)S(1)} %collective-permute-done.1.x_ref, f32[16,512]{1,0:T(8,128)S(1)} %get-tuple-element.32.t_ref, bf16[512,512]{1,0:T(8,128)(2,1)S(1)} %copy-done.5, bf16[256,256]{1,0:T(8,128)(2,1)S(1)} %copy-done.6), custom_call_target="tpu_custom_call" | custom-call | flops 2147483648 | bytes 4194304 | tf_op jit(solution)/shard_map/whiten_across/pallas_call | solution.py:100
  159.3 1.3 copy-done.4
  160.7 3.1 %copy.41 = bf16[256,32,128]{2,1,0:T(8,128)(2,1)S(1)} copy(bf16[256,32,128]{2,0,1:T(8,128)(2,1)} %all-gather.2.cloned.1.call-done) | data formatting | bytes 4194304 | tf_op jit(solution)/shard_map/optimization_barrier | solution.py:279
  163.8 0.1 collective-permute-start.5
  163.9 4.1 %collective-permute-done.5 = bf16[256,32,128]{2,1,0:T(8,128)(2,1)S(1)} collective-permute-done((bf16[256,32,128]{2,1,0:T(8,128)(2,1)S(1)}, bf16[256,32,128]{2,1,0:T(8,128)(2,1)S(1)}, u32[]{:S(2)}, u32[]{:S(2)}) %collective-permute-start.5) | collective-permute-done | bytes 2097184 | tf_op jit(solution)/shard_map/ppermute | solution.py:280
  168.0 1.3 broadcast_select_fusion.1
  169.4 3.5 %pad_maximum_fusion.refs_3_ = bf16[256,64,128]{2,1,0:T(8,128)(2,1)} fusion(bf16[256,32,128]{2,1,0:T(8,128)(2,1)S(1)} %get-tuple-element.20, bf16[256,32,128]{2,1,0:T(8,128)(2,1)S(1)} %get-tuple-element.19), kind=kLoop, calls=%fused_computation | loop fusion | flops 8388608 | bytes 8388608 | tf_op jit(solution)/shard_map/concatenate | solution.py:283
  172.9 26.8 %cross_lags.1 = bf16[128,64,256]{2,1,0:T(8,128)(2,1)} custom-call(bf16[256,2,32,128]{3,2,1,0:T(8,128)(2,1)} %copy-done.2, bf16[256,2,16,128]{3,2,1,0:T(8,128)(2,1)} %copy-done.4, bf16[256,2,16,128]{3,2,1,0:T(8,128)(2,1)} %copy-done.3, bf16[256,64,128]{2,1,0:T(8,128)(2,1)} %pad_maximum_fusion.refs_3_, bf16[256,512]{1,0:T(8,128)(2,1)} %constant.76.clone.refs_4_), custom_call_target="tpu_custom_call" | custom-call | tf_op jit(solution)/shard_map/cross_lags/pallas_call | solution.py:201
  (16 shorter events, 0.1 us)
Async XLA Ops:
  6.5 83.8 %reduce-scatter.2.cloned.1.call-start = ((), (), s32[]{:S(2)}) async-start(), calls=%async_computation.1 | async-start | bytes 2359296 | tf_op jit(solution)/shard_map/reduce_scatter | solution.py:260
  7.5 2.2 %copy-start = (bf16[128,32,512]{2,1,0:T(8,128)(2,1)S(1)}, bf16[128,32,512]{2,1,0:T(8,128)(2,1)}, u32[]{:S(2)}) copy-start(bf16[128,32,512]{2,1,0:T(8,128)(2,1)} %x_ref.5) | copy-start | bytes 12582916
  11.2 4.4 %collective-permute-start = (bf16[64,32,512]{2,1,0:T(8,128)(2,1)S(1)}, bf16[64,32,512]{2,1,0:T(8,128)(2,1)}, u32[]{:S(2)}, u32[]{:S(2)}) collective-permute-start(bf16[64,32,512]{2,1,0:T(8,128)(2,1)S(1)} %pick.3), channel_id=1, source_target_pairs={{0,2},{2,0},{4,6},{6,4},{8,10},{10,8},{12,14},{14,12},{16,18},{18,... | collective-permute-start | bytes 6291464 | tf_op jit(solution)/shard_map/ppermute | solution.py:258
  11.9 2.2 %copy-start.1 = (bf16[128,32,512]{2,1,0:T(8,128)(2,1)S(1)}, bf16[128,32,512]{2,1,0:T(8,128)(2,1)}, u32[]{:S(2)}) copy-start(bf16[128,32,512]{2,1,0:T(8,128)(2,1)} %x_ref.5) | copy-start | bytes 12582916
  19.5 7.8 %copy-start.14 = (s32[32]{0:T(128)S(1)}, s32[32]{0:T(128)}, u32[]{:S(2)}) copy-start(s32[32]{0:T(128)} %param.19) | copy-start | bytes 388
  19.5 7.8 %copy-start.10 = (f32[512]{0:T(512)S(1)}, f32[512]{0:T(512)}, u32[]{:S(2)}) copy-start(f32[512]{0:T(512)} %constant.73.clone) | copy-start | bytes 6148
  19.6 7.8 %copy-start.11 = (f32[512]{0:T(512)S(1)}, f32[512]{0:T(512)}, u32[]{:S(2)}) copy-start(f32[512]{0:T(512)} %constant.72.clone) | copy-start | bytes 6148
  19.6 7.8 %copy-start.12 = (f32[512]{0:T(512)S(1)}, f32[512]{0:T(512)}, u32[]{:S(2)}) copy-start(f32[512]{0:T(512)} %constant.71.clone) | copy-start | bytes 6148
  19.6 7.8 %copy-start.13 = (f32[512]{0:T(512)S(1)}, f32[512]{0:T(512)}, u32[]{:S(2)}) copy-start(f32[512]{0:T(512)} %constant.70.clone) | copy-start | bytes 6148
  19.6 7.9 %copy-start.5 = (bf16[512,512]{1,0:T(8,128)(2,1)S(1)}, bf16[512,512]{1,0:T(8,128)(2,1)}, u32[]{:S(2)}) copy-start(bf16[512,512]{1,0:T(8,128)(2,1)} %constant.74.clone.dft_ref) | copy-start | bytes 1572868
  19.6 7.9 %copy-start.6 = (bf16[256,256]{1,0:T(8,128)(2,1)S(1)}, bf16[256,256]{1,0:T(8,128)(2,1)}, u32[]{:S(2)}) copy-start(bf16[256,256]{1,0:T(8,128)(2,1)} %constant.75.clone.band_ref) | copy-start | bytes 393220
  19.6 141.1 %all-gather.2.cloned.1.call-start = ((), (), s32[]{:S(2)}) async-start(), calls=%async_computation.2 | async-start | bytes 2359296 | tf_op jit(solution)/shard_map/all_gather | solution.py:276
  24.5 49.0 %collective-permute-start.1 = (bf16[128,16,512]{2,1,0:T(8,128)(2,1)}, bf16[128,16,512]{2,1,0:T(8,128)(2,1)S(1)}, u32[]{:S(2)}, u32[]{:S(2)}) collective-permute-start(bf16[128,16,512]{2,1,0:T(8,128)(2,1)} %get-tuple-element.22), channel_id=1, source_target_pairs={{0,1},{1,0},{2,3},{3,2},{4,5},{5,4},{6,7},{7,6},{8,9},{9,8},{10,11... | collective-permute-start | bytes 6291464 | tf_op jit(solution)/shard_map/ppermute | solution.py:231
  27.5 62.8 %copy-start.8 = (bf16[512,512,1]{1,0,2:T(8,128)(2,1)S(1)}, bf16[512,512,1]{1,0,2:T(8,128)(2,1)}, u32[]{:S(2)}) copy-start(bf16[512,512,1]{1,0,2:T(8,128)(2,1)} %constant.77) | copy-start | bytes 1572868
  27.5 64.1 %copy-start.9 = (bf16[256,256,1]{1,0,2:T(8,128)(2,1)S(1)}, bf16[256,256,1]{1,0,2:T(8,128)(2,1)}, u32[]{:S(2)}) copy-start(bf16[256,256,1]{1,0,2:T(8,128)(2,1)} %constant.78) | copy-start | bytes 393220
  44.7 2.0 copy-start.2
  92.1 5.0 %collective-permute-start.2 = (bf16[256,4,2,32]{0,3,2,1:T(8,128)(2,1)S(1)}, bf16[256,4,2,32]{0,3,2,1:T(8,128)(2,1)S(1)}, u32[]{:S(2)}, u32[]{:S(2)}) collective-permute-start(bf16[256,4,2,32]{0,3,2,1:T(8,128)(2,1)S(1)} %get-tuple-element.26), channel_id=1, source_target_pairs={{0,1},{1,0},{2,3},{3,2},{4,5},{5,4},{6,7},{7,6},{8,9},{9,8},{10,11... | collective-permute-start | bytes 393224 | tf_op jit(solution)/shard_map/ppermute | solution.py:231
  98.0 45.1 %collective-permute-start.4 = (bf16[128,16,512]{2,1,0:T(8,128)(2,1)}, bf16[128,16,512]{2,1,0:T(8,128)(2,1)S(1)}, u32[]{:S(2)}, u32[]{:S(2)}) collective-permute-start(bf16[128,16,512]{2,1,0:T(8,128)(2,1)} %get-tuple-element.21), channel_id=1, source_target_pairs={{0,1},{1,0},{2,3},{3,2},{4,5},{5,4},{6,7},{7,6},{8,9},{9,8},{10,11... | collective-permute-start | bytes 6291464 | tf_op jit(solution)/shard_map/ppermute | solution.py:231
  99.3 43.7 %collective-permute-start.3 = (s32[32]{0:T(128)S(1)}, s32[32]{0:T(128)S(1)}, u32[]{:S(2)}, u32[]{:S(2)}) collective-permute-start(s32[32]{0:T(128)S(1)} %copy-done.14), channel_id=1, source_target_pairs={{0,1},{1,0},{2,3},{3,2},{4,5},{5,4},{6,7},{7,6},{8,9},{9,8},{10,11... | collective-permute-start | bytes 392 | tf_op jit(solution)/shard_map/ppermute | solution.py:231
  150.5 1.4 copy-start.3
  159.3 1.4 copy-start.4
  160.7 7.3 %copy-start.7 = (bf16[256,32,128]{2,0,1:T(8,128)(2,1)S(1)}, bf16[256,32,128]{2,0,1:T(8,128)(2,1)}, u32[]{:S(2)}) copy-start(bf16[256,32,128]{2,0,1:T(8,128)(2,1)} %all-gather.2.cloned.1.call-done) | copy-start | bytes 6291460
  163.8 4.2 %collective-permute-start.5 = (bf16[256,32,128]{2,1,0:T(8,128)(2,1)S(1)}, bf16[256,32,128]{2,1,0:T(8,128)(2,1)S(1)}, u32[]{:S(2)}, u32[]{:S(2)}) collective-permute-start(bf16[256,32,128]{2,1,0:T(8,128)(2,1)S(1)} %copy.41), channel_id=1, source_target_pairs={{0,2},{2,0},{4,6},{6,4},{8,10},{10,8},{12,14},{14,12},{16,18},{18,... | collective-permute-start | bytes 6291464 | tf_op jit(solution)/shard_map/ppermute | solution.py:280
Sparse Core Ops, SparseCore 0:
  19.7 70.6 reduce-scatter.1
  98.2 48.0 all-gather.1
